TPU v7x, 256 devices: a whole 4x4x8 slice. The times are simulated.
256 devices in a mesh: reader: 128 (over z, x_lo, y, core), segment: 2 (over x_hi).
Axes of the slice: x: 4 (x_hi: 2, x_lo: 2; x = x_hi * 2 + x_lo), y: 4, z: 8, core: 2. Of those that a mesh axis runs over, the one named last changes fastest.
Arguments:
- dec_input: bfloat16 [2048, 16, 16, 512], P('reader'), may hold values from -6 to 6
- out_cotangent: bfloat16 [2048, 16, 16, 512], P('reader'), may hold values from -6 to 6
- pooled_skip: bfloat16 [2048, 8, 8, 256], P('reader'), may hold values from -6 to 6
- deep_input: bfloat16 [2048, 8, 8, 512], P('reader'), may hold values from -6 to 6
- dec_weight: bfloat16 [9, 64, 64], replicated, may hold values from -0.25 to 0.25
- deep_weight: bfloat16 [27, 128, 128], replicated, may hold values from -0.109375 to 0.109375
- up_weight: bfloat16 [128, 64], replicated, may hold values from -0.5 to 0.5
- down_weight: bfloat16 [64, 128], replicated, may hold values from -0.75 to 0.75
- counts: int32 [128], replicated, may hold values from 2 to 16, as said below
Outputs:
- skip_grad: bfloat16 [2048, 16, 16, 512], P('reader', 'segment')
- dec_weight_grad: float32 [9, 64, 64], replicated
- deep_weight_grad: float32 [27, 128, 128], replicated
- up_weight_grad: float32 [128, 64], replicated
- down_weight_grad: float32 [64, 128], replicated
Inputs may be any that keep to these rules, and one draw needn't show every extreme that they name: `counts`: each reader holds between 2 and 16 occupied blocks, in its first slots; some reader holds 16 and some holds 2.
All inputs are finite; a program needn't handle non-finite values.
Results may differ from a plain program's by a relative error of at most 0.0069.
Values may be sent and summed in bfloat16 or wider, within the bound.
No kernel may reach another device: no remote copies, remote signals or barrier semaphores. Data moves between devices by JAX's collectives and lax.ppermute only.
A program may use at most 128 MiB of HBM per device.

v0:
```python
import math

import jax
import jax.numpy as jnp
from jax import lax
from jax.sharding import PartitionSpec as P

C0 = 64
C1 = 128
BX = 16
BY = 16
BZ = 8


TAPS_FLAT = [(shift_x, shift_y, 0) for shift_x in (-1, 0, 1) for shift_y in (-1, 0, 1)]
TAPS_CUBE = [
    (shift_x, shift_y, shift_z)
    for shift_x in (-1, 0, 1)
    for shift_y in (-1, 0, 1)
    for shift_z in (-1, 0, 1)
]


def from_behind(block, axis, distance):
    devices = range(lax.axis_size(axis))
    route = [(i - distance, i) for i in devices if i - distance in devices]
    return lax.ppermute(block, axis, route)


def gather_taps(volume, tap_list, direction):
    width_x, width_y, width_z = (volume.shape[0], volume.shape[1], volume.shape[2])
    padded = jnp.pad(volume, ((1, 1), (1, 1), (1, 1), (0, 0)))
    pieces = [
        padded[
            1 + direction * shift_x : 1 + direction * shift_x + width_x,
            1 + direction * shift_y : 1 + direction * shift_y + width_y,
            1 + direction * shift_z : 1 + direction * shift_z + width_z,
        ]
        for shift_x, shift_y, shift_z in tap_list
    ]
    return jnp.concatenate(pieces, axis=-1)


def apply_taps(volume, matrix, tap_list, direction):
    stacked = gather_taps(volume, tap_list, direction)
    flattened = stacked.reshape(-1, stacked.shape[-1])
    result = jnp.dot(flattened, matrix, preferred_element_type=jnp.float32)
    return result.reshape(volume.shape[:3] + (matrix.shape[1],))


def weight_taps(volume, gradient, tap_list):
    stacked = gather_taps(volume, tap_list, 1)
    flattened = stacked.reshape(-1, stacked.shape[-1])
    return jnp.dot(
        flattened.T, gradient.reshape(-1, gradient.shape[-1]), preferred_element_type=jnp.float32
    )


def shallow_block(out_block, grad_block, dec_back):
    volume = out_block.reshape(BX, BY, BZ, C0)
    upstream = grad_block.reshape(BX, BY, BZ, C0)
    rectified = jnp.maximum(volume, jnp.zeros_like(volume))
    weight_part = weight_taps(rectified, upstream, TAPS_FLAT)
    backed = apply_taps(upstream, dec_back, TAPS_FLAT, -1)
    skip_total = (
        upstream.astype(jnp.float32) + jnp.where(volume > 0, backed, jnp.float32(0.0))
    ).astype(jnp.bfloat16)
    coarse = (
        skip_total.astype(jnp.float32)
        .reshape(BX // 2, 2, BY // 2, 2, BZ // 2, 2, C0)
        .sum(axis=(1, 3, 5))
        .astype(jnp.bfloat16)
    )
    return (
        skip_total.reshape(BX, BY, BZ * C0),
        coarse.reshape(BX // 2, BY // 2, BZ // 2 * C0),
        weight_part,
    )


def deep_block(coarse_grad, pooled_block, saved_deep, deep_fwd, deep_back, up_back, down_back):
    upstream = coarse_grad.reshape(-1, C0)
    start_vol = saved_deep.reshape(BX // 2, BY // 2, BZ // 2, C1)
    rectified = jnp.maximum(start_vol, jnp.zeros_like(start_vol))
    deep_out = (
        start_vol.astype(jnp.float32) + apply_taps(rectified, deep_fwd, TAPS_CUBE, 1)
    ).astype(jnp.bfloat16)
    up_part = jnp.dot(deep_out.reshape(-1, C1).T, upstream, preferred_element_type=jnp.float32)
    deep_grad = jnp.dot(upstream, up_back, preferred_element_type=jnp.float32).astype(jnp.bfloat16)
    deep_grad = deep_grad.reshape(BX // 2, BY // 2, BZ // 2, C1)
    deep_part = weight_taps(rectified, deep_grad, TAPS_CUBE)
    backed = apply_taps(deep_grad, deep_back, TAPS_CUBE, -1)
    input_grad = (
        deep_grad.astype(jnp.float32) + jnp.where(start_vol > 0, backed, jnp.float32(0.0))
    ).astype(jnp.bfloat16)
    flat_input = input_grad.reshape(-1, C1)
    down_part = jnp.dot(
        pooled_block.reshape(-1, C0).T, flat_input, preferred_element_type=jnp.float32
    )
    pool_grad = jnp.dot(flat_input, down_back, preferred_element_type=jnp.float32).astype(
        jnp.bfloat16
    )
    return (pool_grad.reshape(BX // 2, BY // 2, BZ // 2 * C0), deep_part, up_part, down_part)


def expand_coarse(coarse):
    number = coarse.shape[0]
    rows_x = coarse.shape[1]
    spread_out = coarse.astype(jnp.float32).reshape(number, rows_x, 1, BY // 2, 1, BZ // 2, 1, C0)
    spread_out = jnp.broadcast_to(spread_out, (number, rows_x, 2, BY // 2, 2, BZ // 2, 2, C0))
    return spread_out.reshape(number, 2 * rows_x, BY, BZ * C0)


def finish(fine_half, coarse):
    return (fine_half.astype(jnp.float32) + 0.125 * expand_coarse(coarse)).astype(jnp.bfloat16)


def pick_row(source, row_id):
    return lax.dynamic_index_in_dim(source, row_id, 0, False)


def per_device(
    dec_input,
    out_cotangent,
    pooled_skip,
    deep_input,
    dec_weight,
    deep_weight,
    up_weight,
    down_weight,
    counts,
):
    segment_idx = lax.axis_index("segment")
    reader_idx = lax.axis_index("reader")
    readers = lax.axis_size("reader")
    own_count = counts[reader_idx]
    slot_total = dec_input.shape[0]
    dec_back = dec_weight.transpose(0, 2, 1).reshape(9 * C0, C0)
    deep_fwd = deep_weight.reshape(27 * C1, C1)
    deep_back = deep_weight.transpose(0, 2, 1).reshape(27 * C1, C1)
    up_back = up_weight.T
    down_back = down_weight.T
    work_fine, work_grad, work_pool, work_deep = (dec_input, out_cotangent, pooled_skip, deep_input)
    work_rows = work_fine.shape[0]
    is_shallow = segment_idx == 0
    shallow_start = (
        jnp.zeros(work_fine.shape, jnp.bfloat16),
        jnp.zeros((work_rows, BX // 2, BY // 2, BZ // 2 * C0), jnp.bfloat16),
        jnp.zeros((9 * C0, C0), jnp.float32),
    )

    def shallow_phase():

        def shallow_advance(position, totals):
            skip_rows, coarse_rows, dec_total = totals
            skip_block, coarse_block, dec_piece = shallow_block(
                pick_row(work_fine, position), pick_row(work_grad, position), dec_back
            )
            skip_rows = lax.dynamic_update_index_in_dim(skip_rows, skip_block, position, 0)
            coarse_rows = lax.dynamic_update_index_in_dim(coarse_rows, coarse_block, position, 0)
            return (skip_rows, coarse_rows, dec_total + dec_piece)

        return lax.fori_loop(0, own_count, shallow_advance, shallow_start)

    def shallow_rest():
        return shallow_start

    skip_rows, coarse_rows, dec_part = lax.cond(is_shallow, shallow_phase, shallow_rest)
    got_coarse, got_upper = from_behind((coarse_rows, skip_rows[:, BX // 2 :]), "segment", 1)
    deep_start = (
        jnp.zeros((work_rows, BX // 2, BY // 2, BZ // 2 * C0), jnp.bfloat16),
        got_upper,
        jnp.zeros((27 * C1, C1), jnp.float32),
        jnp.zeros((C1, C0), jnp.float32),
        jnp.zeros((C0, C1), jnp.float32),
    )

    def deep_phase():

        def deep_advance(position, totals):
            coarse_back, upper_half, deep_total, up_total, down_total = totals
            back_block, deep_piece, up_piece, down_piece = deep_block(
                pick_row(got_coarse, position),
                pick_row(work_pool, position),
                pick_row(work_deep, position),
                deep_fwd,
                deep_back,
                up_back,
                down_back,
            )
            coarse_back = lax.dynamic_update_index_in_dim(coarse_back, back_block, position, 0)
            return (
                coarse_back,
                upper_half,
                deep_total + deep_piece,
                up_total + up_piece,
                down_total + down_piece,
            )

        return lax.fori_loop(0, own_count, deep_advance, deep_start)

    def deep_rest():
        return deep_start

    coarse_back, upper_half, deep_part, up_part, down_part = lax.cond(
        segment_idx == 1, deep_phase, deep_rest
    )
    lower_coarse = from_behind(coarse_back[:, : BX // 4], "segment", -1)
    base_rows = jnp.where(is_shallow, skip_rows[:, : BX // 2], upper_half)
    coarse_part = jnp.where(is_shallow, lower_coarse, coarse_back[:, BX // 4 :])
    finished = finish(base_rows, coarse_part)
    slot_ids = jnp.arange(slot_total, dtype=jnp.int32)
    skip_grad = jnp.where(
        (slot_ids < own_count)[:, None, None, None], finished, jnp.zeros_like(finished)
    )
    dec_sum, deep_sum, up_sum, down_sum = lax.psum(
        (dec_part, deep_part, up_part, down_part), ("reader", "segment")
    )
    grad_scale = 1.0 / math.sqrt(readers * slot_total * BX * BY * BZ)
    return (
        skip_grad,
        (dec_sum * grad_scale).reshape(9, C0, C0),
        (deep_sum * grad_scale).reshape(27, C1, C1),
        up_sum * grad_scale,
        down_sum * grad_scale,
    )


def solution(mesh):
    return jax.shard_map(
        per_device,
        mesh=mesh,
        in_specs=(
            P("reader", None, None, None),
            P("reader", None, None, None),
            P("reader", None, None, None),
            P("reader", None, None, None),
            P(),
            P(),
            P(),
            P(),
            P(),
        ),
        out_specs=(P("reader", "segment", None, None), P(), P(), P(), P()),
        check_vma=False,
    )
```

profile of v0, /device:TPU:1, one launch (start us, length us, event | category | flops | bytes accessed | tf_op | source)
XLA Modules:
  0.0 1366.7 jit_solution(18244815661711109265)
XLA Ops:
  8.3 1.3 dynamic_slice.36
  9.6 158.0 %conditional.2 = (bf16[16,16,16,512]{3,2,1,0:T(8,128)(2,1)}, bf16[16,8,8,256]{3,2,1,0:T(8,128)(2,1)}, f32[576,64]{0,1:T(8,128)}) conditional(s32[]{:T(128)} %convert_element_type.97, () %tuple.48, (bf16[9,64,64]{2,1,0:T(8,128)(2,1)S(1)}, s32[]{:T(128)}, bf16[16,16,16,512]{3,2,1,0:T(8,128)(2,1)}, bf16[16,16,16,512]{3,2,1,0:T(8,128)(2,1)}) %tuple.110), branch_computations={%region_0.0_spmd, %region_1.5_spmd} | conditional | flops 303321088 | bytes 30974284 | solution.py:168
  10.3 2.5 broadcast_in_dim.63
  14.3 153.3 %while.32 = (s32[]{:T(128)}, bf16[16,16,16,512]{3,2,1,0:T(8,128)(2,1)}, bf16[16,8,8,256]{3,2,1,0:T(8,128)(2,1)}, f32[576,64]{0,1:T(8,128)}, s32[]{:T(128)}, /*in...) while((s32[]{:T(128)}, ...), condition=%wide.region_4.4_spmd, body=%wide.region_2.3_spmd.sunk | while | flops 303321088 | bytes 25960644 | solution.py:163
  16.2 2.4 pad_slice_fusion.70
  18.6 5.2 concatenate.31
  25.9 2.7 fusion.65
  28.6 1.4 broadcast_in_dim.90
  30.0 1.8 dynamic-slice_maximum_fusion.2
  32.0 2.4 pad_slice_fusion.71
  34.4 5.2 concatenate.32
  39.6 1.1 reshape.283
  40.7 2.4 convolution_add_fusion.12
  46.8 2.4 pad_slice_fusion.70
  49.2 5.2 concatenate.31
  56.5 2.7 fusion.65
  59.1 1.4 broadcast_in_dim.90
  60.5 1.8 dynamic-slice_maximum_fusion.2
  62.5 2.4 pad_slice_fusion.71
  65.0 5.2 concatenate.32
  70.2 1.1 reshape.283
  71.2 2.3 convolution_add_fusion.12
  77.3 2.4 pad_slice_fusion.70
  79.7 5.2 concatenate.31
  87.0 2.7 fusion.65
  89.7 1.4 broadcast_in_dim.90
  91.0 1.8 dynamic-slice_maximum_fusion.2
  93.1 2.4 pad_slice_fusion.71
  95.5 5.2 concatenate.32
  100.7 1.1 reshape.283
  101.8 2.3 convolution_add_fusion.12
  107.9 2.4 pad_slice_fusion.70
  110.3 5.2 concatenate.31
  117.6 2.7 fusion.65
  120.2 1.4 broadcast_in_dim.90
  121.6 1.7 dynamic-slice_maximum_fusion.2
  123.6 2.4 pad_slice_fusion.71
  126.0 5.2 concatenate.32
  131.2 1.1 reshape.283
  132.3 2.4 convolution_add_fusion.12
  138.4 2.4 pad_slice_fusion.70
  140.8 5.2 concatenate.31
  148.1 2.7 fusion.65
  150.7 1.4 broadcast_in_dim.90
  152.1 1.7 dynamic-slice_maximum_fusion.2
  154.1 2.4 pad_slice_fusion.71
  156.5 5.2 concatenate.32
  162.8 2.4 convolution_add_fusion.12
  167.6 2.1 collective-permute-start.1
  169.8 2.2 copy.34
  172.7 2.7 collective-permute-done.1
  175.4 3.4 conditional.3
  175.4 1.3 broadcast_in_dim.65
  179.6 3.1 slice.452
  182.7 111.4 %collective-permute-start = (bf16[16,8,16,512]{3,2,1,0:T(8,128)(2,1)}, bf16[16,8,16,512]{3,2,1,0:T(8,128)(2,1)}, u32[]{:S(2)}, u32[]{:S(2)}) collective-permute-start(bf16[16,8,16,512]{3,2,1,0:T(8,128)(2,1)} %slice.452), channel_id=1, source_target_pairs={{0,1},{2,3},{4,5},{6,7},{8,9},{10,11},{12,13},{14,15},{16,17},{18,... | collective-permute-start | bytes 6291464 | tf_op jit(solution)/shard_map/ppermute | solution.py:27
  295.7 1.3 collective-permute-start.2
  297.0 790.9 %all-reduce.9.cloned.1.call-done = (f32[128,64]{0,1:T(8,128)}, f32[64,128]{1,0:T(8,128)}) async-done(((f32[128,64]{0,1:T(8,128)}, f32[64,128]{1,0:T(8,128)}), (f32[128,64]{0,1:T(8,128)}, f32[64,128]{1,0:T(8,128)})) %all-reduce.9.cloned.1.call-update) | async-done | bytes 65552 | tf_op jit(solution)/shard_map/psum | solution.py:216
  1087.9 1.4 broadcast_multiply_fusion.2
  1089.3 1.4 broadcast_multiply_fusion.3
  1092.2 6.1 broadcast_in_dim.77
  1098.3 10.8 mul.40
  1109.1 240.7 %all-reduce.11.cloned.1.call-done = (f32[576,64]{0,1:T(8,128)}, f32[3456,128]{1,0:T(8,128)}) async-done(((f32[576,64]{0,1:T(8,128)}, f32[3456,128]{1,0:T(8,128)}), (f32[576,64]{0,1:T(8,128)}, f32[3456,128]{1,0:T(8,128)})) %all-reduce.11.cloned.1.call-update) | async-done | bytes 1916944 | tf_op jit(solution)/shard_map/psum | solution.py:216
  1351.6 2.8 broadcast_multiply_fusion
  1354.4 5.4 fusion.8
  (75 shorter events, 39.7 us)
Async XLA Ops:
  7.2 1080.8 %all-reduce.9.cloned.1.call-start = ((), (), s32[]{:S(2)}) async-start(), calls=%async_computation | async-start | bytes 131072 | tf_op jit(solution)/shard_map/psum | solution.py:216
  40.7 2.4 copy-start
  71.2 2.4 copy-start
  101.8 2.4 copy-start
  132.3 2.4 copy-start
  162.8 2.4 copy-start
  167.6 4.4 copy-start.5
  167.6 7.7 copy-start.4
  167.6 7.7 collective-permute-start.1
  178.8 1171.0 %all-reduce.11.cloned.1.call-start = ((), (), s32[]{:S(2)}) async-start(), calls=%async_computation.1 | async-start | bytes 3866624 | tf_op jit(solution)/shard_map/psum | solution.py:216
  182.7 1171.7 %collective-permute-start = (bf16[16,8,16,512]{3,2,1,0:T(8,128)(2,1)}, bf16[16,8,16,512]{3,2,1,0:T(8,128)(2,1)}, u32[]{:S(2)}, u32[]{:S(2)}) collective-permute-start(bf16[16,8,16,512]{3,2,1,0:T(8,128)(2,1)} %slice.452), channel_id=1, source_target_pairs={{0,1},{2,3},{4,5},{6,7},{8,9},{10,11},{12,13},{14,15},{16,17},{18,... | collective-permute-start | bytes 6291464 | tf_op jit(solution)/shard_map/ppermute | solution.py:27
  295.7 795.0 %collective-permute-start.2 = (bf16[16,4,8,256]{3,2,1,0:T(8,128)(2,1)S(1)}, bf16[16,4,8,256]{3,2,1,0:T(8,128)(2,1)S(1)}, u32[]{:S(2)}, u32[]{:S(2)}) collective-permute-start(bf16[16,4,8,256]{3,2,1,0:T(8,128)(2,1)S(1)} %slice.453), channel_id=1, source_target_pairs={{1,0},{3,2},{5,4},{7,6},{9,8},{11,10},{13,12},{15,14},{17,16},{19,... | collective-permute-start | bytes 786440 | tf_op jit(solution)/shard_map/ppermute | solution.py:27
Sparse Core Ops, SparseCore 0:
  178.9 908.9 all-reduce.8
  1094.0 255.7 all-reduce.10
where the time goes:
time: 1380 us; the launch traced here: 1370 us
  waiting for transfers between devices  1040 us (75%)
  local copies, waits for them, and re-layouts  141 us (10%)
  starting transfers between devices  115 us (8%)
  other arithmetic  32.7 us (2%)
  matrix products  25 us (2%)
  between operations  14.1 us (1%)
    psum x2, waiting for transfers between devices, per_device(): lax.psum((dec_part, deep_part, up_part, down_part), ('reader', 'segment'))  1030 us
    ppermute x3, starting transfers between devices, from_behind(): return lax.ppermute(block, axis, route)  115 us
    concatenate x10, local copies, waits for them, and re-layouts, gather_taps(): return jnp.concatenate(pieces, axis=-1)  52.1 us
  transfers between devices with their start and end apart: 5, of which 3 were waited for; matrix products, arithmetic and copies ran while one was open for 2% of the time, Pallas kernels for 0%

commit v1 on v0

v1 whole, which is shorter than its diff:
```python
import functools
import math

import jax
import jax.numpy as jnp
from jax import lax
from jax.experimental import pallas as pl
from jax.experimental.pallas import tpu as pltpu
from jax.sharding import Mesh, PartitionSpec as P

C0 = 64
C1 = 128
BX = 16
BY = 16
BZ = 8
F32 = jnp.float32
BF16 = jnp.bfloat16
OFFS = (-1, 0, 1)


def cat(parts, axis):
    return parts[0] if len(parts) == 1 else jnp.concatenate(parts, axis=axis)


def lanes(index, width=128):
    return slice(index * width, (index + 1) * width)


def shift_rows(value, distance, keep):
    rows = value.shape[0]
    return jnp.where(keep, pltpu.roll(value, distance % rows, 0), F32(0.0))


def dot(lhs, rhs):
    return jnp.dot(lhs, rhs, preferred_element_type=F32)


def shallow_kernel(
    info_ref, grad_ref, out_ref, wpair_ref, skip_ref, coarse_ref, dec_ref,
    shifted, turned, toeplitz, spread, total,
):
    step = pl.program_id(0)
    half = info_ref[0]
    count = info_ref[1]
    sign = 1 - 2 * half

    @pl.when(step == 0)
    def _():
        for dyi in range(3):
            for b in range(2):
                shifted[dyi, b, 0] = jnp.zeros((BY, 512), BF16)
        turned[0] = jnp.zeros((128, 128), BF16)
        for w in range(4):
            for dyi in range(3):
                for xi in range(2):
                    dxf = 1 + xi - w
                    if abs(dxf) <= 1:
                        block = wpair_ref[3 * (dxf * sign + 1) + dyi]
                    else:
                        block = jnp.zeros((128, 128), BF16)
                    toeplitz[lanes(3 * w + dyi), lanes(xi)] = block
        total[...] = jnp.zeros_like(total)

    row_id = lax.broadcasted_iota(jnp.int32, (BY, 512), 0)
    not_first = row_id > 0
    not_last = row_id < BY - 1
    for b in range(2):
        live = 2 * step + b < count
        for i in range(11):
            value = grad_ref[b, half * 15 + sign * i].astype(F32)
            value = jnp.where(live, value, F32(0.0))
            shifted[0, b, i + 1] = shift_rows(value, -1, not_last).astype(BF16)
            shifted[1, b, i + 1] = value.astype(BF16)
            shifted[2, b, i + 1] = shift_rows(value, 1, not_first).astype(BF16)

    for i in range(9):
        parts = []
        for b in range(2):
            row = out_ref[b, half * 15 + sign * i]
            row = jnp.maximum(row, jnp.zeros_like(row))
            parts += [row[:, lanes(z)] for z in range(4)]
        turned[i + 1] = cat(parts, 0).T

    lhs = cat([cat([turned[i + dxi] for i in range(8)], 1) for dxi in range(3)], 0)
    rhs = cat(
        [
            cat([shifted[dyi, b, i + 1, :, lanes(z)] for dyi in range(3)], 1)
            for i in range(8)
            for b in range(2)
            for z in range(4)
        ],
        0,
    )
    total[...] += dot(lhs, rhs)

    lhs = cat(
        [
            cat(
                [
                    shifted[dyi, b, 2 * xp + w, :, lanes(z)]
                    for b in range(2)
                    for xp in range(5)
                    for z in range(4)
                ],
                0,
            )
            for w in range(4)
            for dyi in range(3)
        ],
        1,
    )
    backed = dot(lhs, toeplitz[...])
    low_lane = lax.broadcasted_iota(jnp.int32, (8, 128), 1) < 64
    for xp in range(5):
        pooled = []
        for b in range(2):
            both = []
            for xi in range(2):
                i = 2 * xp + xi
                base = (b * 5 + xp) * 64
                conv = cat([backed[base + 16 * z : base + 16 * z + 16, lanes(xi)] for z in range(4)], 1)
                gate = out_ref[b, half * 15 + sign * i].astype(F32) > 0
                value = shifted[1, b, i + 1].astype(F32) + jnp.where(gate, conv, F32(0.0))
                value = value.astype(BF16)
                if i < 8:
                    skip_ref[b, half * 7 + sign * i] = value
                both.append(value.astype(F32))
            cell = both[0] + both[1]
            cell = cat(
                [cell[:, lanes(z)] + pltpu.roll(cell[:, lanes(z)], 64, 1) for z in range(4)], 1
            )
            quads = []
            for z in range(4):
                spread[b, z] = cell[:, lanes(z)]
                even = spread[b, z, pl.ds(0, 8, stride=2), :]
                quads.append(even + spread[b, z, pl.ds(1, 8, stride=2), :])
            pooled.append(
                cat([jnp.where(low_lane, quads[2 * k], quads[2 * k + 1]) for k in range(2)], 1)
            )
        coarse_ref[xp] = cat(pooled, 0).astype(BF16)

    @pl.when(step == pl.num_programs(0) - 1)
    def _():
        low = lax.broadcasted_iota(jnp.int32, (64, 128), 1) < 64
        low_half = lax.broadcasted_iota(jnp.int32, (32, 128), 1) < 64
        for dxi in range(3):
            for dyi in range(3):
                block = total[lanes(dxi), lanes(dyi)]
                other = pltpu.roll(block, 64, 1)
                summed = jnp.where(low, block[:64] + other[64:], block[64:] + other[:64])
                tap = 3 * ((dxi - 1) * sign + 1) + dyi
                dec_ref[tap] = jnp.where(low_half, summed[:32], summed[32:])


def deep_kernel(
    info_ref, coarse_ref, pooled_ref, deep_ref, weight_ref, upt_ref, downt_ref,
    part_ref, upart_ref, dpart_ref, pool_grad_ref,
    start, rect, grads, pools, turned, wfwd, wback, up_mat, down_mat,
):
    half = info_ref[0]
    sign = 1 - 2 * half

    row_id = lax.broadcasted_iota(jnp.int32, (128, 512), 0) % 8
    not_first = row_id > 0
    not_last = row_id < 7

    for dyi in range(3):
        rect[dyi, 0] = jnp.zeros((128, 512), BF16)
        grads[dyi, 0] = jnp.zeros((128, 512), BF16)
    for z in range(4):
        turned[0, z] = jnp.zeros((128, 128), BF16)

    for i in range(5):
        source = half * 7 + sign * i
        for p in range(8):
            pair = cat([deep_ref[2 * p + b, source].astype(F32) for b in range(2)], 0)
            start[i, 16 * p : 16 * p + 16] = pair.astype(BF16)
            if i < 4:
                pair = cat([pooled_ref[2 * p + b, source].astype(F32) for b in range(2)], 0)
                pools[i, 16 * p : 16 * p + 16] = pair.astype(BF16)
        value = jnp.maximum(start[i].astype(F32), F32(0.0))
        rect[0, i + 1] = shift_rows(value, 1, not_first).astype(BF16)
        rect[1, i + 1] = value.astype(BF16)
        rect[2, i + 1] = shift_rows(value, -1, not_last).astype(BF16)
        for z in range(4):
            turned[i + 1, z] = rect[1, i + 1, :, lanes(z)].T

    zero = jnp.zeros((128, 128), BF16)
    for dxi in range(3):
        for dyi in range(3):
            tap = 9 * ((dxi - 1) * sign + 1) + 3 * dyi
            plain = [weight_ref[tap + k] for k in range(3)]
            flipped = [value.T for value in plain]
            for g in range(2):
                for zi in range(3):
                    for zo in range(2):
                        dz = (zi + g) - (zo + 2 * g)
                        rows = lanes((3 * dxi + dyi) * 3 + zi)
                        wfwd[g, rows, lanes(zo)] = plain[dz + 1] if abs(dz) <= 1 else zero
                        wback[g, rows, lanes(zo)] = flipped[1 - dz] if abs(dz) <= 1 else zero

    up_mat[...] = jnp.zeros_like(up_mat)
    down_mat[...] = jnp.zeros_like(down_mat)
    for z in range(4):
        up_mat[lanes(z, 64), lanes(z)] = upt_ref[...]
        down_mat[lanes(z), lanes(z)] = downt_ref[...]

    coarse = cat([coarse_ref[i] for i in range(5)], 0)
    grad = dot(coarse, up_mat[...])
    for i in range(5):
        value = grad[lanes(i)].astype(BF16).astype(F32)
        grads[0, i + 1] = shift_rows(value, -1, not_last).astype(BF16)
        grads[1, i + 1] = value.astype(BF16)
        grads[2, i + 1] = shift_rows(value, 1, not_first).astype(BF16)

    for dzi in range(3):
        dz = dzi - 1
        levels = [z for z in range(4) if 0 <= z + dz < 4]
        lhs = cat(
            [
                cat([turned[i + dxi, z + dz] for z in levels for i in range(4)], 1)
                for dxi in range(3)
            ],
            0,
        )
        rhs = cat(
            [
                cat([grads[dyi, i + 1, :, lanes(z)] for dyi in range(3)], 1)
                for z in levels
                for i in range(4)
            ],
            0,
        )
        part = dot(lhs, rhs)
        for dxi in range(3):
            for dyi in range(3):
                tap = 9 * ((dxi - 1) * sign + 1) + 3 * dyi + dzi
                part_ref[tap] = part[lanes(dxi), lanes(dyi)]

    outs = []
    for g in range(2):
        wide = slice(g * 128, g * 128 + 384)
        lhs = cat(
            [
                cat([rect[dyi, i + dxi, :, wide] for i in range(4)], 0)
                for dxi in range(3)
                for dyi in range(3)
            ],
            1,
        )
        conv = dot(lhs, wfwd[g])
        first = cat([start[i, :, lanes(g, 256)] for i in range(4)], 0).astype(F32)
        outs.append((first + conv).astype(BF16))
    coarse_t = cat([coarse_ref[i].T for i in range(4)], 1)
    full = dot(coarse_t, cat(outs, 1))
    upart_ref[...] = sum(full[lanes(z, 64), lanes(z)] for z in range(4))

    outs = []
    for g in range(2):
        wide = slice(g * 128, g * 128 + 384)
        lhs = cat(
            [
                cat([grads[dyi, i + 2 - dxi, :, wide] for i in range(4)], 0)
                for dxi in range(3)
                for dyi in range(3)
            ],
            1,
        )
        conv = dot(lhs, wback[g])
        first = cat([start[i, :, lanes(g, 256)] for i in range(4)], 0).astype(F32)
        base = cat([grads[1, i + 1, :, lanes(g, 256)] for i in range(4)], 0).astype(F32)
        outs.append((base + jnp.where(first > 0, conv, F32(0.0))).astype(BF16))
    input_grad = cat(outs, 1)
    pools_t = cat([pools[i].T for i in range(4)], 1)
    full = dot(pools_t, input_grad)
    dpart_ref[...] = sum(full[lanes(z, 64), lanes(z)] for z in range(4))
    pool_grad = dot(input_grad, down_mat[...]).astype(BF16)
    for i in range(4):
        pool_grad_ref[i] = pool_grad[lanes(i)]


def finish_kernel(info_ref, skip_ref, pool_ref, done_ref, spread):
    half = info_ref[0]
    sign = 1 - 2 * half
    for i in range(4):
        coarse = pool_ref[i].astype(F32) * F32(0.125)
        for b in range(2):
            value = coarse[8 * b : 8 * b + 8]
            for z in range(4):
                spread[b, z, pl.ds(0, 8, stride=2), :] = value[:, lanes(z)]
                spread[b, z, pl.ds(1, 8, stride=2), :] = value[:, lanes(z)]
            wide = cat([spread[b, z] for z in range(4)], 1)
            for xi in range(2):
                row = half * 7 + sign * (2 * i + xi)
                done_ref[b, row] = (skip_ref[b, row].astype(F32) + wide).astype(BF16)


def pair_blocks(weight):
    back = weight.transpose(0, 2, 1)
    zero = jnp.zeros_like(back)
    return jnp.concatenate(
        [jnp.concatenate([back, zero], 2), jnp.concatenate([zero, back], 2)], 1
    )


def local_work(half, count, dec_input, out_cotangent, pooled_skip, deep_input, dec_weight, deep_weight, up_weight, down_weight):
    info = jnp.stack([half, count]).astype(jnp.int32)
    slots = dec_input.shape[0]
    params = dict(vmem_limit_bytes=48 * 1024 * 1024)

    def whole(*shape):
        return pl.BlockSpec(shape, lambda s, info: (0,) * len(shape))

    fine = pl.BlockSpec((2, BX, BY, 512), lambda s, info: (s, 0, 0, 0))
    skip, coarse, dec_part = pl.pallas_call(
        shallow_kernel,
        grid_spec=pltpu.PrefetchScalarGridSpec(
            num_scalar_prefetch=1,
            grid=(slots // 2,),
            in_specs=[fine, fine, whole(9, 128, 128)],
            out_specs=[
                pl.BlockSpec((2, 8, BY, 512), lambda s, info: (s, 0, 0, 0)),
                pl.BlockSpec((5, 16, 256), lambda s, info: (0, s, 0)),
                whole(9, 32, 128),
            ],
            scratch_shapes=[
                pltpu.VMEM((3, 2, 12, BY, 512), BF16),
                pltpu.VMEM((10, 128, 128), BF16),
                pltpu.VMEM((1536, 256), BF16),
                pltpu.VMEM((2, 4, BY, 128), F32),
                pltpu.VMEM((384, 384), F32),
            ],
        ),
        out_shape=[
            jax.ShapeDtypeStruct((slots, 8, BY, 512), BF16),
            jax.ShapeDtypeStruct((5, slots * 8, 256), BF16),
            jax.ShapeDtypeStruct((9, 32, 128), F32),
        ],
        compiler_params=pltpu.CompilerParams(**params),
        name="shallow",
    )(info, out_cotangent, dec_input, pair_blocks(dec_weight))

    up_t = up_weight.T
    down_t = jnp.concatenate([down_weight.T, down_weight.T], 1)
    deep_part, up_part, down_part, pool_grad = pl.pallas_call(
        deep_kernel,
        grid_spec=pltpu.PrefetchScalarGridSpec(
            num_scalar_prefetch=1,
            grid=(1,),
            in_specs=[
                whole(5, 128, 256),
                whole(16, 8, 8, 256),
                whole(16, 8, 8, 512),
                whole(27, 128, 128),
                whole(64, 128),
                whole(128, 128),
            ],
            out_specs=[whole(27, 128, 128), whole(64, 128), whole(64, 128), whole(4, 128, 512)],
            scratch_shapes=[
                pltpu.VMEM((5, 128, 512), BF16),
                pltpu.VMEM((3, 6, 128, 512), BF16),
                pltpu.VMEM((3, 6, 128, 512), BF16),
                pltpu.VMEM((4, 128, 256), BF16),
                pltpu.VMEM((6, 4, 128, 128), BF16),
                pltpu.VMEM((2, 3456, 256), BF16),
                pltpu.VMEM((2, 3456, 256), BF16),
                pltpu.VMEM((256, 512), BF16),
                pltpu.VMEM((512, 512), BF16),
            ],
        ),
        out_shape=[
            jax.ShapeDtypeStruct((27, 128, 128), F32),
            jax.ShapeDtypeStruct((64, 128), F32),
            jax.ShapeDtypeStruct((64, 128), F32),
            jax.ShapeDtypeStruct((4, 128, 512), BF16),
        ],
        compiler_params=pltpu.CompilerParams(**params),
        name="deep",
    )(info, coarse, pooled_skip, deep_input, deep_weight, up_t, down_t)

    skip_grad = pl.pallas_call(
        finish_kernel,
        grid_spec=pltpu.PrefetchScalarGridSpec(
            num_scalar_prefetch=1,
            grid=(slots // 2,),
            in_specs=[
                pl.BlockSpec((2, 8, BY, 512), lambda s, info: (s, 0, 0, 0)),
                pl.BlockSpec((4, 16, 512), lambda s, info: (0, s, 0)),
            ],
            out_specs=pl.BlockSpec((2, 8, BY, 512), lambda s, info: (s, 0, 0, 0)),
            scratch_shapes=[pltpu.VMEM((2, 4, BY, 128), F32)],
        ),
        out_shape=jax.ShapeDtypeStruct((slots, 8, BY, 512), BF16),
        compiler_params=pltpu.CompilerParams(**params),
        name="finish",
    )(info, skip, pool_grad)
    return skip_grad, dec_part, deep_part, up_part, down_part


AXES = ("z", "xl", "y", "core", "xh")
READER = ("z", "xl", "y", "core")
PLANE = ("xl", "y", "xh")


def scatter_sum(rows, axes, parts):
    split = rows.reshape(parts, -1, 128)
    split = lax.all_to_all(split, axes, 0, 0, tiled=True)
    return split.sum(axis=0)


def gather(rows, axes, parts):
    copies = jnp.broadcast_to(rows[None], (parts,) + rows.shape)
    return lax.all_to_all(copies, axes, 0, 0, tiled=True).reshape(-1, 128)


def sum_everywhere(rows):
    core = lax.axis_index("core")
    swap = [(0, 1), (1, 0)]
    halves = rows.reshape(2, -1, 128)
    mine = lax.dynamic_index_in_dim(halves, core, 0, False)
    other = lax.dynamic_index_in_dim(halves, 1 - core, 0, False)
    mine = mine + lax.ppermute(other, "core", swap)
    mine = scatter_sum(mine, PLANE, 16)
    mine = scatter_sum(mine, "z", 8)
    mine = gather(mine.astype(BF16), "z", 8)
    mine = gather(mine, PLANE, 16)
    other = lax.ppermute(mine, "core", swap)
    low = jnp.where(core == 0, mine, other)
    high = jnp.where(core == 0, other, mine)
    return jnp.concatenate([low, high], axis=0).astype(F32)


def per_device(
    dec_input, out_cotangent, pooled_skip, deep_input,
    dec_weight, deep_weight, up_weight, down_weight, counts,
):
    reader = lax.axis_index(READER)
    half = lax.axis_index("xh")
    slots = dec_input.shape[0]
    skip_grad, dec_part, deep_part, up_part, down_part = local_work(
        half, counts[reader], dec_input, out_cotangent, pooled_skip, deep_input,
        dec_weight, deep_weight, up_weight, down_weight,
    )
    rows = jnp.concatenate(
        [deep_part.reshape(-1, 128), dec_part.reshape(-1, 128), up_part, down_part,
         jnp.zeros((224, 128), F32)], axis=0,
    )
    scale = 1.0 / math.sqrt(counts.shape[0] * slots * BX * BY * BZ)
    rows = sum_everywhere(rows) * scale
    deep_sum = rows[:3456].reshape(27, C1, C1)
    dec_sum = rows[3456:3744].reshape(9, 32, 128)
    dec_sum = jnp.concatenate([dec_sum[..., :64], dec_sum[..., 64:]], axis=1)
    up_sum = rows[3744:3808].T
    down_sum = rows[3808:3872]
    return skip_grad, dec_sum, deep_sum, up_sum, down_sum


def solution(mesh):
    fine = Mesh(mesh.devices.reshape(8, 2, 4, 2, 2), AXES)
    spec = P(READER, None, None, None)
    return jax.shard_map(
        per_device,
        mesh=fine,
        in_specs=(spec, spec, spec, spec, P(), P(), P(), P(), P()),
        out_specs=(P(READER, "xh", None, None), P(), P(), P(), P()),
        check_vma=False,
    )
```

time: 1380 us -> 112 us (0.08)
  waiting for transfers between devices: 1040 us -> 2.63 us
  local copies, waits for them, and re-layouts: 141 us -> 11.4 us
  starting transfers between devices: 115 us -> 8.68 us
  blocking collectives: 0 us -> 57.1 us
  other arithmetic: 32.7 us -> 5.87 us
  Pallas kernels: 0 us -> 25.1 us
  matrix products: 25 us -> 0 us
    psum x2 -> x0, waiting for transfers between devices: 1030 us -> none  [per_device(): lax.psum((dec_part, deep_part, up_part, down_part), ('reader', 'segment'))]
    ppermute x3 -> x2, starting transfers between devices: 115 us -> 8.68 us  [the longest x1 5.47 us: sum_everywhere(): other = lax.ppermute(mine, 'core', swap)]
    all_to_all x0 -> x4, blocking collectives: none -> 57.1 us  [the longest x2 35.4 us: scatter_sum(): split = lax.all_to_all(split, axes, 0, 0, tiled=True)]
    concatenate x10 -> x1, local copies, waits for them, and re-layouts: 52.1 us -> 0.65 us  [per_device(): jnp.concatenate([deep_part.reshape(-1, 128), dec_part.reshape(-1, 128), u...]
    slice x12 -> x4, local copies, waits for them, and re-layouts: 28.3 us -> 2.06 us  [the longest x1 1.32 us: per_device(): deep_sum = rows[:3456].reshape(27, C1, C1)]
    pallas_call x0 -> x3, Pallas kernels: none -> 25.1 us  [the longest x1 12.9 us: local_work(): pl.pallas_call(shallow_kernel, grid_spec=pltpu.PrefetchScalarGridSpec(num...]
    dot_general x10 -> x0, matrix products: 25 us -> none  [the longest x5 13.3 us: apply_taps(): result = jnp.dot(flattened, matrix, preferred_element_type=jnp.float32)]
    broadcast_in_dim x11 -> x2, local copies, waits for them, and re-layouts: 18.7 us -> 0.1 us  [gather(): copies = jnp.broadcast_to(rows[None], (parts,) + rows.shape)]
  transfers between devices with their start and end apart: 5 -> 2, of which waited for: 3 -> 1; matrix products, arithmetic and copies ran while one was open for 2% -> 0% of each run, Pallas kernels for 0% -> 3%
where the time goes in v1:
time: 112 us
  blocking collectives  57.1 us (51%)
  Pallas kernels  25.1 us (22%)
  local copies, waits for them, and re-layouts  11.4 us (10%)
  starting transfers between devices  8.68 us (8%)
  other arithmetic  5.87 us (5%)
  waiting for transfers between devices  2.63 us (2%)
    all_to_all x2, blocking collectives, scatter_sum(): split = lax.all_to_all(split, axes, 0, 0, tiled=True)  35.4 us
    all_to_all x2, blocking collectives, gather(): return lax.all_to_all(copies, axes, 0, 0, tiled=True).reshape(-1, 128)  21.8 us
    pallas_call x1, Pallas kernels, local_work(): pl.pallas_call(shallow_kernel, grid_spec=pltpu.PrefetchScalarGridSpec(num...  12.9 us
    pallas_call x1, Pallas kernels, local_work(): pl.pallas_call(deep_kernel, grid_spec=pltpu.PrefetchScalarGridSpec(num_sc...  8.47 us
    ppermute x1, starting transfers between devices, sum_everywhere(): other = lax.ppermute(mine, 'core', swap)  5.47 us
    unnamed x14, local copies, waits for them, and re-layouts  5.11 us
    pallas_call x1, Pallas kernels, local_work(): pl.pallas_call(finish_kernel, grid_spec=pltpu.PrefetchScalarGridSpec(num_...  3.75 us
    ppermute x1, starting transfers between devices, sum_everywhere(): mine = mine + lax.ppermute(other, 'core', swap)  3.21 us
  transfers between devices with their start and end apart: 2, of which 1 were waited for; matrix products, arithmetic and copies ran while one was open for 0% of the time, Pallas kernels for 3%

profile of v1, /device:TPU:1, one launch (start us, length us, event | category | flops | bytes accessed | tf_op | source)
XLA Modules:
  0.0 111.6 jit_solution(5437046676363927120)
XLA Ops:
  0.6 1.0 copy.16
  1.7 0.1 fusion.2.wpair_ref
  1.8 0.8 copy.17
  2.6 0.1 pad_maximum_fusion.1.downt_ref
  2.7 1.2 %dynamic_slice.10 = s32[1]{0:T(128)} dynamic-slice(s32[128]{0:T(128)} %param.17, s32[]{:T(128)S(6)} %select_n.22), dynamic_slice_sizes={1} | dynamic-slice | bytes 12 | tf_op jit(solution)/shard_map/dynamic_slice | solution.py:441
  4.0 0.7 pad_add_fusion.info_ref
  4.7 0.0 copy-start
  4.7 0.0 copy-start.1
  4.7 0.0 copy-start.2
  4.7 0.0 copy-start.3
  4.7 12.9 %shallow.1 = (bf16[16,8,16,512]{3,2,1,0:T(8,128)(2,1)S(1)}, bf16[5,128,256]{2,1,0:T(8,128)(2,1)S(1)}, f32[9,32,128]{2,1,0:T(8,128)S(1)}) custom-call(s32[2]{0:T(128)S(1)} %pad_add_fusion.info_ref, bf16[16,16,16,512]{3,2,1,0:T(8,128)(2,1)} %grad_ref.1, bf16[16,16,16,512]{3,2,1,0:T(8,128)(2,1)} %out_ref.1, bf16[9,128,128]{2,1,0:T(8,128)(2,1)S(1)} %fusion.2.wpair_ref), custom_call_target="tpu_custom_call" | custom-call | tf_op jit(solution)/shard_map/shallow/pallas_call | solution.py:315
  17.6 0.0 copy-done
  17.6 0.0 copy-done.1
  17.6 0.0 copy-done.2
  17.6 0.0 copy-done.3
  17.7 8.5 %deep.1 = (f32[27,128,128]{2,1,0:T(8,128)S(1)}, f32[64,128]{1,0:T(8,128)S(1)}, f32[64,128]{1,0:T(8,128)S(1)}, bf16[4,128,512]{2,1,0:T(8,128)(2,1)S(1)}) custom-call(s32[2]{0:T(128)S(1)} %pad_add_fusion.info_ref, bf16[5,128,256]{2,1,0:T(8,128)(2,1)S(1)} %get-tuple-element.13.coarse_ref, bf16[16,8,8,256]{3,2,1,0:T(8,128)(2,1)S(1)} %copy-done.2, ...), custom_call_target="tpu_custom_call" | custom-call | tf_op jit(solution)/shard_map/deep/pallas_call | solution.py:345
  26.1 1.3 %constant_dynamic-update-slice_fusion.3 = f32[4096,128]{1,0:T(8,128)} fusion(f32[3456,128]{1,0:T(8,128)S(1)} %bitcast.21), kind=kLoop, calls=%fused_computation.17 | loop fusion | bytes 3538944
  27.5 0.7 constant_dynamic-update-slice_fusion.2
  28.1 0.6 constant_dynamic-update-slice_fusion.1
  28.7 0.6 constant_dynamic-update-slice_fusion
  29.4 0.7 broadcast_dynamic-update-slice_fusion
  30.0 2.3 %dynamic-slice_bitcast_fusion = f32[2048,128]{1,0:T(8,128)} fusion(f32[2,2048,128]{2,1,0:T(8,128)} %bitcast.6, s32[]{:T(128)S(6)} %select_n.25), kind=kLoop, calls=%fused_computation.2 | loop fusion | bytes 2097156 | tf_op jit(solution)/shard_map/jit(dynamic_index_in_dim)/squeeze | solution.py:421
  32.3 3.2 %collective-permute-start = (f32[2048,128]{1,0:T(8,128)}, f32[2048,128]{1,0:T(8,128)}, u32[]{:S(2)}, u32[]{:S(2)}) collective-permute-start(f32[2048,128]{1,0:T(8,128)} %dynamic-slice_bitcast_fusion), channel_id=1, source_target_pairs={{0,2},{2,0},{1,3},{3,1},{4,6},{6,4},{5,7},{7,5},{8,10},{10,8},{9,1... | collective-permute-start | bytes 3145736 | tf_op jit(solution)/shard_map/ppermute | solution.py:422
  35.5 2.6 %collective-permute-done = f32[2048,128]{1,0:T(8,128)} collective-permute-done((f32[2048,128]{1,0:T(8,128)}, f32[2048,128]{1,0:T(8,128)}, u32[]{:S(2)}, u32[]{:S(2)}) %collective-permute-start) | collective-permute-done | bytes 1048608 | tf_op jit(solution)/shard_map/ppermute | solution.py:422
  38.1 1.6 %bitcast_add_fusion = f32[2048,128]{1,0:T(8,128)S(1)} fusion(f32[2048,128]{1,0:T(8,128)} %collective-permute-done, f32[2,2048,128]{2,1,0:T(8,128)} %bitcast.6, s32[]{:T(128)S(6)} %select_n.24), kind=kLoop, calls=%fused_computation.1 | loop fusion | flops 262144 | bytes 3145732 | tf_op jit(solution)/shard_map/add | solution.py:422
  39.8 20.1 %all_to_all.20 = f32[16,128,128]{2,1,0:T(8,128)} all-to-all(f32[16,128,128]{2,1,0:T(8,128)S(1)} %bitcast.24), channel_id=1, replica_groups=mesh['z'=8,'xl'=2,'y'=4,'core'=2,'xh'=2] {'xl','y','xh'}, dimensions={0} | all-to-all | bytes 2097152 | tf_op jit(solution)/shard_map/all_to_all | solution.py:407
  59.8 1.3 %reduce_sum.18 = f32[128,128]{1,0:T(8,128)S(1)} reduce(f32[16,128,128]{2,1,0:T(8,128)} %all_to_all.20, f32[]{:T(128)} %constant.44.clone.1), dimensions={0}, to_apply=%region_0.1 | reduce | flops 245760 | bytes 1114116 | tf_op jit(solution)/shard_map/reduce_sum | solution.py:408
  61.1 15.3 %all_to_all.21 = f32[8,16,128]{2,1,0:T(8,128)S(1)} all-to-all(f32[8,16,128]{2,1,0:T(8,128)S(1)} %bitcast.29), channel_id=1, replica_groups=mesh['z'=8,'xl'=2,'y'=4,'core'=2,'xh'=2] {'z'}, dimensions={0} | all-to-all | bytes 131072 | tf_op jit(solution)/shard_map/all_to_all | solution.py:407
  76.5 9.2 %all_to_all.22 = bf16[8,16,128]{2,1,0:T(8,128)(2,1)S(1)} all-to-all(bf16[8,16,128]{2,1,0:T(8,128)(2,1)S(1)} %broadcast_in_dim.18), channel_id=1, replica_groups=mesh['z'=8,'xl'=2,'y'=4,'core'=2,'xh'=2] {'z'}, dimensions={0} | all-to-all | bytes 65536 | tf_op jit(solution)/shard_map/all_to_all | solution.py:413
  85.7 0.1 broadcast_in_dim.20
  85.8 12.5 %all_to_all.23 = bf16[16,128,128]{2,1,0:T(8,128)(2,1)S(1)} all-to-all(bf16[16,128,128]{2,1,0:T(8,128)(2,1)S(1)} %broadcast_in_dim.20), channel_id=1, replica_groups=mesh['z'=8,'xl'=2,'y'=4,'core'=2,'xh'=2] {'xl','y','xh'}, dimensions={0} | all-to-all | bytes 1048576 | tf_op jit(solution)/shard_map/all_to_all | solution.py:413
  98.3 5.5 %collective-permute-start.1 = (bf16[2048,128]{1,0:T(8,128)(2,1)S(1)}, bf16[2048,128]{1,0:T(8,128)(2,1)}, u32[]{:S(2)}, u32[]{:S(2)}) collective-permute-start(bf16[2048,128]{1,0:T(8,128)(2,1)S(1)} %bitcast.25), channel_id=1, source_target_pairs={{0,2},{2,0},{1,3},{3,1},{4,6},{6,4},{5,7},{7,5},{8,10},{10,8},{9,1... | collective-permute-start | bytes 1572872 | tf_op jit(solution)/shard_map/ppermute | solution.py:427
  103.8 3.7 %finish.1 = bf16[16,8,16,512]{3,2,1,0:T(8,128)(2,1)} custom-call(s32[2]{0:T(128)S(1)} %pad_add_fusion.info_ref, bf16[16,8,16,512]{3,2,1,0:T(8,128)(2,1)S(1)} %get-tuple-element.12.skip_ref, bf16[4,128,512]{2,1,0:T(8,128)(2,1)S(1)} %get-tuple-element.14.pool_ref), custom_call_target="tpu_custom_call" | custom-call | tf_op jit(solution)/shard_map/finish/pallas_call | solution.py:381
  107.5 0.0 collective-permute-done.1
  107.5 1.1 broadcast_select_fusion.1
  108.7 0.1 convert_multiply_fusion
  108.8 1.3 %slice.27 = f32[3456,128]{1,0:T(8,128)} slice(f32[4096,128]{1,0:T(8,128)S(1)} %convert_multiply_fusion), slice={[0:3456], [0:128]} | slice | bytes 3538944 | tf_op jit(solution)/shard_map/slice | solution.py:450
  110.2 0.6 fusion.3
  110.8 0.1 fusion.4
  110.9 0.7 pad_maximum_fusion
  (3 shorter events, 0.0 us)
Async XLA Ops:
  4.7 12.9 %copy-start = (bf16[16,8,8,512]{3,2,1,0:T(8,128)(2,1)S(1)}, bf16[16,8,8,512]{3,2,1,0:T(8,128)(2,1)}, u32[]{:S(2)}) copy-start(bf16[16,8,8,512]{3,2,1,0:T(8,128)(2,1)} %deep_ref.1) | copy-start | bytes 3145732
  4.7 12.9 %copy-start.1 = (bf16[27,128,128]{2,1,0:T(8,128)(2,1)S(1)}, bf16[27,128,128]{2,1,0:T(8,128)(2,1)}, u32[]{:S(2)}) copy-start(bf16[27,128,128]{2,1,0:T(8,128)(2,1)} %weight_ref.1) | copy-start | bytes 2654212
  4.7 12.9 %copy-start.2 = (bf16[16,8,8,256]{3,2,1,0:T(8,128)(2,1)S(1)}, bf16[16,8,8,256]{3,2,1,0:T(8,128)(2,1)}, u32[]{:S(2)}) copy-start(bf16[16,8,8,256]{3,2,1,0:T(8,128)(2,1)} %pooled_ref.1) | copy-start | bytes 1572868
  4.7 12.9 %copy-start.3 = (bf16[128,64]{0,1:T(8,128)(2,1)S(1)}, bf16[128,64]{0,1:T(8,128)(2,1)}, u32[]{:S(2)}) copy-start(bf16[128,64]{0,1:T(8,128)(2,1)} %param.15) | copy-start | bytes 49156
  32.3 5.8 %collective-permute-start = (f32[2048,128]{1,0:T(8,128)}, f32[2048,128]{1,0:T(8,128)}, u32[]{:S(2)}, u32[]{:S(2)}) collective-permute-start(f32[2048,128]{1,0:T(8,128)} %dynamic-slice_bitcast_fusion), channel_id=1, source_target_pairs={{0,2},{2,0},{1,3},{3,1},{4,6},{6,4},{5,7},{7,5},{8,10},{10,8},{9,1... | collective-permute-start | bytes 3145736 | tf_op jit(solution)/shard_map/ppermute | solution.py:422
  98.3 9.2 %collective-permute-start.1 = (bf16[2048,128]{1,0:T(8,128)(2,1)S(1)}, bf16[2048,128]{1,0:T(8,128)(2,1)}, u32[]{:S(2)}, u32[]{:S(2)}) collective-permute-start(bf16[2048,128]{1,0:T(8,128)(2,1)S(1)} %bitcast.25), channel_id=1, source_target_pairs={{0,2},{2,0},{1,3},{3,1},{4,6},{6,4},{5,7},{7,5},{8,10},{10,8},{9,1... | collective-permute-start | bytes 1572872 | tf_op jit(solution)/shard_map/ppermute | solution.py:427

commit v2 on v0

v2 whole, which is shorter than its diff:
```python
import math

import jax
import jax.numpy as jnp
from jax import lax
from jax.experimental import pallas as pl
from jax.experimental.pallas import tpu as pltpu
from jax.sharding import Mesh, PartitionSpec as P

C0 = 64
C1 = 128
BX = 16
BY = 16
BZ = 8
F32 = jnp.float32
BF16 = jnp.bfloat16

AXES = ("zh", "zl", "xl", "y", "core", "xh")
READER = ("zh", "zl", "xl", "y", "core")
NEAR = ("zl", "xl", "y", "xh")
FAR = "zh"
UNITS = 16


def cat(parts, axis):
    return parts[0] if len(parts) == 1 else jnp.concatenate(parts, axis=axis)


def lanes(index, width=128):
    return slice(index * width, (index + 1) * width)


def shift_rows(value, distance, keep):
    rows = value.shape[0]
    return jnp.where(keep, pltpu.roll(value, distance % rows, 0), F32(0.0))


def dot(lhs, rhs):
    return jnp.dot(lhs, rhs, preferred_element_type=F32)


def unit_of(dyi, dzi):
    first = 9 * dzi + 3 * dyi
    return (0, first) if first < 15 else (1, first - 15)


def work_kernel(
    counts_ref, grad_ref, out_ref, deep_ref, pooled_ref, wdec_ref, wdeep_ref, wup_ref, wdown_ref,
    skip_ref, pool_grad_ref, mine_ref, other_ref,
    shifted, turned, toeplitz, spread, total, tile, parts,
    start, rect, grads, pools, coarse, deep_turned, wfwd, wback, up_mat, down_mat, sems,
):
    step = pl.program_id(0)
    last = pl.num_programs(0) - 1
    half = lax.axis_index("xh")
    core = lax.axis_index("core")
    count = counts_ref[lax.axis_index(READER)]
    sign = 1 - 2 * half

    @pl.when(step == 0)
    def _():
        tile[...] = jnp.zeros_like(tile)
        low_lane = lax.broadcasted_iota(jnp.int32, (64, 128), 1) < 64
        backs = []
        for tap in range(9):
            tile[:64, :64] = wdec_ref[tap].astype(F32)
            upper = jnp.where(low_lane, tile[:64], F32(0.0))
            backs.append(cat([upper, pltpu.roll(upper, 64, 1)], 0).T.astype(BF16))
            turned_pair = backs[tap]
            parts[0, tap, :64] = turned_pair[:64].astype(F32)
            parts[0, tap, 64:] = turned_pair[64:].astype(F32)
        for w in range(4):
            for dyi in range(3):
                for xi in range(2):
                    dxf = 1 + xi - w
                    if abs(dxf) <= 1:
                        block = parts[0, 3 * (dxf * sign + 1) + dyi].astype(BF16)
                    else:
                        block = jnp.zeros((128, 128), BF16)
                    toeplitz[lanes(3 * w + dyi), lanes(xi)] = block
        total[...] = jnp.zeros_like(total)
        parts[1, UNITS - 1] = jnp.zeros((128, 128), F32)
        for dyi in range(3):
            for b in range(2):
                shifted[dyi, b, 0] = jnp.zeros((BY, 512), BF16)
            rect[dyi, 0] = jnp.zeros((128, 512), BF16)
            grads[dyi, 0] = jnp.zeros((128, 512), BF16)
        turned[0] = jnp.zeros((128, 128), BF16)
        for z in range(4):
            deep_turned[0, z] = jnp.zeros((128, 128), BF16)
        up_mat[...] = jnp.zeros_like(up_mat)
        down_mat[...] = jnp.zeros_like(down_mat)
        down = wdown_ref[...].astype(F32)
        down_t = cat([down, down], 0).T.astype(BF16)
        for z in range(4):
            up_mat[lanes(z, 64), lanes(z)] = wup_ref[...]
            down_mat[lanes(z), lanes(z)] = down_t

    def deep_weights():
        group = 3 * ((step // 3 - 1) * sign + 1) + step % 3
        zero = jnp.zeros((128, 128), BF16)
        plain = [wdeep_ref[k] for k in range(3)]
        flipped = [value.T for value in plain]
        for zi in range(3):
            rows = pl.ds(pl.multiple_of((group * 3 + zi) * 128, 128), 128)
            for g in range(2):
                for zo in range(2):
                    dz = (zi + g) - (zo + 2 * g)
                    wfwd[g, rows, lanes(zo)] = plain[dz + 1] if abs(dz) <= 1 else zero
                    wback[g, rows, lanes(zo)] = flipped[1 - dz] if abs(dz) <= 1 else zero

    @pl.when(step < last)
    def _():
        deep_weights()
        row_id = lax.broadcasted_iota(jnp.int32, (BY, 512), 0)
        not_first = row_id > 0
        not_last = row_id < BY - 1
        deep_first = row_id % 8 > 0
        deep_last = row_id % 8 < 7
        rows = pl.ds(pl.multiple_of(step * 16, 16), 16)
        for b in range(2):
            live = 2 * step + b < count
            for i in range(11):
                value = grad_ref[b, half * 15 + sign * i].astype(F32)
                value = jnp.where(live, value, F32(0.0))
                shifted[0, b, i + 1] = shift_rows(value, -1, not_last).astype(BF16)
                shifted[1, b, i + 1] = value.astype(BF16)
                shifted[2, b, i + 1] = shift_rows(value, 1, not_first).astype(BF16)
        for i in range(9):
            tiles = []
            for b in range(2):
                row = out_ref[b, half * 15 + sign * i]
                row = jnp.maximum(row, jnp.zeros_like(row))
                tiles += [row[:, lanes(z)] for z in range(4)]
            turned[i + 1] = cat(tiles, 0).T

        lhs = cat(
            [
                cat(
                    [
                        shifted[dyi, b, 2 * xp + w, :, lanes(z)]
                        for b in range(2)
                        for xp in range(5)
                        for z in range(4)
                    ],
                    0,
                )
                for w in range(4)
                for dyi in range(3)
            ],
            1,
        )
        backed = dot(lhs, toeplitz[...])

        lhs = cat([cat([turned[i + dxi] for i in range(8)], 1) for dxi in range(3)], 0)
        rhs = cat(
            [
                cat([shifted[dyi, b, i + 1, :, lanes(z)] for dyi in range(3)], 1)
                for i in range(8)
                for b in range(2)
                for z in range(4)
            ],
            0,
        )
        total[...] += dot(lhs, rhs)

        for i in range(5):
            source = half * 7 + sign * i
            value = cat([deep_ref[b, source].astype(F32) for b in range(2)], 0)
            start[i, rows] = value.astype(BF16)
            value = jnp.maximum(value, F32(0.0))
            rect[0, i + 1, rows] = shift_rows(value, 1, deep_first).astype(BF16)
            rect[1, i + 1, rows] = value.astype(BF16)
            rect[2, i + 1, rows] = shift_rows(value, -1, deep_last).astype(BF16)
            if i < 4:
                value = cat([pooled_ref[b, source].astype(F32) for b in range(2)], 0)
                pools[i, rows] = value.astype(BF16)

        low_lane = lax.broadcasted_iota(jnp.int32, (8, 128), 1) < 64
        for xp in range(5):
            pooled = []
            for b in range(2):
                both = []
                for xi in range(2):
                    i = 2 * xp + xi
                    base = (b * 5 + xp) * 64
                    conv = cat(
                        [backed[base + 16 * z : base + 16 * z + 16, lanes(xi)] for z in range(4)], 1
                    )
                    gate = out_ref[b, half * 15 + sign * i].astype(F32) > 0
                    value = shifted[1, b, i + 1].astype(F32) + jnp.where(gate, conv, F32(0.0))
                    value = value.astype(BF16)
                    if i < 8:
                        skip_ref[b, half * 7 + sign * i] = value
                    both.append(value.astype(F32))
                cell = both[0] + both[1]
                quads = []
                for z in range(4):
                    piece = cell[:, lanes(z)]
                    slot = (xp * 2 + b) * 4 + z
                    spread[slot] = piece + pltpu.roll(piece, 64, 1)
                    even = spread[slot, pl.ds(0, 8, stride=2), :]
                    quads.append(even + spread[slot, pl.ds(1, 8, stride=2), :])
                pooled.append(
                    cat(
                        [jnp.where(low_lane, quads[2 * k], quads[2 * k + 1]) for k in range(2)], 1
                    )
                )
            coarse[xp, rows] = cat(pooled, 0).astype(BF16)

    @pl.when(step == last)
    def _():
        deep_weights()
        row_id = lax.broadcasted_iota(jnp.int32, (128, 512), 0) % 8
        not_first = row_id > 0
        not_last = row_id < 7

        grad = dot(cat([coarse[i] for i in range(5)], 0), up_mat[...])
        for i in range(5):
            value = grad[lanes(i)].astype(BF16).astype(F32)
            grads[0, i + 1] = shift_rows(value, -1, not_last).astype(BF16)
            grads[1, i + 1] = value.astype(BF16)
            grads[2, i + 1] = shift_rows(value, 1, not_first).astype(BF16)
            for z in range(4):
                deep_turned[i + 1, z] = rect[1, i + 1, :, lanes(z)].T

        outs = []
        for g in range(2):
            wide = slice(g * 128, g * 128 + 384)
            lhs = cat(
                [
                    cat([rect[dyi, i + dxi, :, wide] for i in range(4)], 0)
                    for dxi in range(3)
                    for dyi in range(3)
                ],
                1,
            )
            conv = dot(lhs, wfwd[g])
            first = cat([start[i, :, lanes(g, 256)] for i in range(4)], 0).astype(F32)
            outs.append((first + conv).astype(BF16))
        coarse_t = cat([coarse[i].T for i in range(4)], 1)
        full = dot(coarse_t, cat(outs, 1))
        parts[0, UNITS - 1, :64] = sum(full[lanes(z, 64), lanes(z)] for z in range(4))

        for dzi in range(3):
            dz = dzi - 1
            levels = [z for z in range(4) if 0 <= z + dz < 4]
            lhs = cat(
                [
                    cat([deep_turned[i + dxi, z + dz] for z in levels for i in range(4)], 1)
                    for dxi in range(3)
                ],
                0,
            )
            rhs = cat(
                [
                    cat([grads[dyi, i + 1, :, lanes(z)] for dyi in range(3)], 1)
                    for z in levels
                    for i in range(4)
                ],
                0,
            )
            part = dot(lhs, rhs)
            for dyi in range(3):
                side, first = unit_of(dyi, dzi)
                for dxi in range(3):
                    parts[side, first + (dxi - 1) * sign + 1] = part[lanes(dxi), lanes(dyi)]

        low = lax.broadcasted_iota(jnp.int32, (64, 128), 1) < 64
        low_half = lax.broadcasted_iota(jnp.int32, (32, 128), 1) < 64
        for dxi in range(3):
            for dyi in range(3):
                block = total[lanes(dxi), lanes(dyi)]
                turned_lanes = pltpu.roll(block, 64, 1)
                summed = jnp.where(
                    low, block[:64] + turned_lanes[64:], block[64:] + turned_lanes[:64]
                )
                summed = jnp.where(low_half, summed[:32], summed[32:])
                row = pl.multiple_of(((dxi - 1) * sign + 1) * 32, 32)
                parts[1, 12 + dyi, pl.ds(row, 32)] = summed
        for dyi in range(3):
            parts[1, 12 + dyi, 96:] = jnp.zeros((32, 128), F32)

        outs = []
        for g in range(2):
            wide = slice(g * 128, g * 128 + 384)
            lhs = cat(
                [
                    cat([grads[dyi, i + 2 - dxi, :, wide] for i in range(4)], 0)
                    for dxi in range(3)
                    for dyi in range(3)
                ],
                1,
            )
            conv = dot(lhs, wback[g])
            first = cat([start[i, :, lanes(g, 256)] for i in range(4)], 0).astype(F32)
            base = cat([grads[1, i + 1, :, lanes(g, 256)] for i in range(4)], 0).astype(F32)
            outs.append((base + jnp.where(first > 0, conv, F32(0.0))).astype(BF16))
        input_grad = cat(outs, 1)
        full = dot(cat([pools[i].T for i in range(4)], 1), input_grad)
        parts[0, UNITS - 1, 64:] = sum(full[lanes(z, 64), lanes(z)] for z in range(4))
        send = pltpu.make_async_copy(parts.at[1 - core], other_ref, sems.at[0])
        keep = pltpu.make_async_copy(parts.at[core], mine_ref, sems.at[1])
        send.start()
        keep.start()
        pool_grad = dot(input_grad, down_mat[...]).astype(BF16)
        for i in range(4):
            pool_grad_ref[i] = pool_grad[lanes(i)]
        send.wait()
        keep.wait()


def finish_kernel(skip_ref, pool_ref, done_ref, spread):
    half = lax.axis_index("xh")
    sign = 1 - 2 * half
    for i in range(4):
        for p in range(2):
            coarse = pool_ref[i, 16 * p : 16 * p + 16].astype(F32) * F32(0.125)
            for b in range(2):
                value = coarse[8 * b : 8 * b + 8]
                wide = []
                for z in range(4):
                    slot = ((i * 2 + p) * 2 + b) * 4 + z
                    spread[slot, pl.ds(0, 8, stride=2), :] = value[:, lanes(z)]
                    spread[slot, pl.ds(1, 8, stride=2), :] = value[:, lanes(z)]
                    wide.append(spread[slot])
                wide = cat(wide, 1)
                for xi in range(2):
                    row = half * 7 + sign * (2 * i + xi)
                    value_in = skip_ref[2 * p + b, row].astype(F32)
                    done_ref[2 * p + b, row] = (value_in + wide).astype(BF16)


def unpack_kernel(mine_ref, other_ref, dec_ref, deep_ref, up_ref, down_ref, *, scale):
    first_half = lax.axis_index("core") == 0

    def unit(side, index):
        rows = lanes(index)
        mine = mine_ref[rows].astype(F32)
        other = other_ref[rows].astype(F32)
        return jnp.where(first_half, *((mine, other) if side == 0 else (other, mine))) * F32(scale)

    for dyi in range(3):
        for dzi in range(3):
            side, first = unit_of(dyi, dzi)
            for dxi in range(3):
                deep_ref[9 * dxi + 3 * dyi + dzi] = unit(side, first + dxi)
        block = unit(1, 12 + dyi)
        for dxi in range(3):
            piece = block[lanes(dxi, 32)]
            dec_ref[3 * dxi + dyi, :32] = piece[:, :64]
            dec_ref[3 * dxi + dyi, 32:] = pltpu.roll(piece, 64, 1)[:, :64]
    block = unit(0, UNITS - 1)
    up_ref[...] = block[:64]
    down_ref[...] = block[64:]


def whole(*shape):
    return pl.BlockSpec(shape, lambda *step: (0,) * len(shape))


def work(counts, dec_input, out_cotangent, pooled_skip, deep_input, dec_weight, deep_weight, up_weight, down_weight):
    slots = dec_input.shape[0]
    steps = slots // 2

    def pair(*shape):
        return pl.BlockSpec(
            (2,) + shape, lambda s, counts: (jnp.minimum(s, steps - 1),) + (0,) * len(shape)
        )

    anywhere = pl.BlockSpec(memory_space=pl.ANY)
    return pl.pallas_call(
        work_kernel,
        grid_spec=pltpu.PrefetchScalarGridSpec(
            num_scalar_prefetch=1,
            grid=(steps + 1,),
            in_specs=[
                pair(BX, BY, 512),
                pair(BX, BY, 512),
                pair(8, 8, 512),
                pair(8, 8, 256),
                whole(9, 64, 64),
                pl.BlockSpec((3, 128, 128), lambda s, counts: (s, 0, 0)),
                whole(64, 128),
                whole(64, 128),
            ],
            out_specs=[pair(8, BY, 512), whole(4, 8 * slots, 512), anywhere, anywhere],
            scratch_shapes=[
                pltpu.VMEM((3, 2, 12, BY, 512), BF16),
                pltpu.VMEM((10, 128, 128), BF16),
                pltpu.VMEM((1536, 256), BF16),
                pltpu.VMEM((40, BY, 128), F32),
                pltpu.VMEM((384, 384), F32),
                pltpu.VMEM((128, 128), F32),
                pltpu.VMEM((2, UNITS, 128, 128), F32),
                pltpu.VMEM((5, 128, 512), BF16),
                pltpu.VMEM((3, 6, 128, 512), BF16),
                pltpu.VMEM((3, 6, 128, 512), BF16),
                pltpu.VMEM((4, 128, 256), BF16),
                pltpu.VMEM((5, 128, 256), BF16),
                pltpu.VMEM((6, 4, 128, 128), BF16),
                pltpu.VMEM((2, 3456, 256), BF16),
                pltpu.VMEM((2, 3456, 256), BF16),
                pltpu.VMEM((256, 512), BF16),
                pltpu.VMEM((512, 512), BF16),
                pltpu.SemaphoreType.DMA((2,)),
            ],
        ),
        out_shape=[
            jax.ShapeDtypeStruct((slots, 8, BY, 512), BF16),
            jax.ShapeDtypeStruct((4, 8 * slots, 512), BF16),
            jax.ShapeDtypeStruct((UNITS, 128, 128), F32),
            jax.ShapeDtypeStruct((UNITS, 128, 128), F32),
        ],
        compiler_params=pltpu.CompilerParams(vmem_limit_bytes=60 * 1024 * 1024),
        name="work",
    )(counts, out_cotangent, dec_input, deep_input, pooled_skip, dec_weight, deep_weight, up_weight.T, down_weight)


def finish(skip, pool_grad):
    slots = skip.shape[0]
    blocks = pl.BlockSpec((4, 8, BY, 512), lambda s: (s, 0, 0, 0))
    return pl.pallas_call(
        finish_kernel,
        grid=(slots // 4,),
        in_specs=[blocks, pl.BlockSpec((4, 32, 512), lambda s: (0, s, 0))],
        out_specs=blocks,
        scratch_shapes=[pltpu.VMEM((64, BY, 128), F32)],
        out_shape=jax.ShapeDtypeStruct(skip.shape, BF16),
        compiler_params=pltpu.CompilerParams(vmem_limit_bytes=12 * 1024 * 1024),
        cost_estimate=pl.CostEstimate(flops=1 << 20, bytes_accessed=1 << 23, transcendentals=0),
        name="finish",
    )(skip, pool_grad)


def scatter_sum(rows, axes):
    split = rows.reshape(lax.axis_size(axes), -1, 128)
    split = lax.all_to_all(split, axes, 0, 0, tiled=True)
    return split.astype(F32).sum(axis=0)


def spread_out(rows, axes):
    copies = jnp.broadcast_to(rows[None], (lax.axis_size(axes),) + rows.shape)
    return lax.all_to_all(copies, axes, 0, 0, tiled=True)


def per_device(
    dec_input, out_cotangent, pooled_skip, deep_input,
    dec_weight, deep_weight, up_weight, down_weight, counts,
):
    slots = dec_input.shape[0]
    swap = [(0, 1), (1, 0)]
    skip, pool_grad, mine, other = work(
        counts, dec_input, out_cotangent, pooled_skip, deep_input,
        dec_weight, deep_weight, up_weight, down_weight,
    )
    other = lax.ppermute(other, "core", swap)
    rows = (mine + other).astype(BF16).reshape(-1, 128)
    rows = scatter_sum(rows, NEAR)
    rows = spread_out(rows, FAR).sum(axis=0).astype(BF16)
    mine = spread_out(rows, NEAR).reshape(-1, 128)
    mine, pool_grad = lax.optimization_barrier((mine, pool_grad))
    other = lax.ppermute(mine, "core", swap)
    skip_grad = finish(skip, pool_grad)
    scale = 1.0 / math.sqrt(counts.shape[0] * slots * BX * BY * BZ)
    dec_sum, deep_sum, up_sum, down_sum = pl.pallas_call(
        lambda *refs: unpack_kernel(*refs, scale=scale),
        out_shape=[
            jax.ShapeDtypeStruct((9, C0, C0), F32),
            jax.ShapeDtypeStruct((27, C1, C1), F32),
            jax.ShapeDtypeStruct((C0, C1), F32),
            jax.ShapeDtypeStruct((C0, C1), F32),
        ],
        compiler_params=pltpu.CompilerParams(vmem_limit_bytes=32 * 1024 * 1024),
        name="unpack",
    )(mine, other)
    return skip_grad, dec_sum, deep_sum, up_sum.T, down_sum


def build(fine):
    spec = P(READER, None, None, None)
    return jax.shard_map(
        per_device,
        mesh=fine,
        in_specs=(spec, spec, spec, spec, P(), P(), P(), P(), P()),
        out_specs=(P(READER, "xh", None, None), P(), P(), P(), P()),
        check_vma=False,
    )


def solution(mesh):
    return build(Mesh(mesh.devices.reshape(4, 2, 2, 4, 2, 2), AXES))
```

time: 1380 us -> 86 us (0.06)
  waiting for transfers between devices: 1040 us -> 2.5 us
  local copies, waits for them, and re-layouts: 141 us -> 0.13 us
  starting transfers between devices: 115 us -> 7.66 us
  blocking collectives: 0 us -> 45.7 us
  other arithmetic: 32.7 us -> 1.43 us
  Pallas kernels: 0 us -> 27.6 us
  matrix products: 25 us -> 0 us
    psum x2 -> x0, waiting for transfers between devices: 1030 us -> none  [per_device(): lax.psum((dec_part, deep_part, up_part, down_part), ('reader', 'segment'))]
    ppermute x3 -> x2, starting transfers between devices: 115 us -> 7.66 us  [the longest x1 4.33 us: per_device(): other = lax.ppermute(mine, 'core', swap)]
    concatenate x10 -> x0, local copies, waits for them, and re-layouts: 52.1 us -> none  [gather_taps(): return jnp.concatenate(pieces, axis=-1)]
    all_to_all x0 -> x3, blocking collectives: none -> 45.7 us  [the longest x2 28.1 us: spread_out(): return lax.all_to_all(copies, axes, 0, 0, tiled=True)]
    slice x12 -> x0, local copies, waits for them, and re-layouts: 28.3 us -> none  [the longest x10 24.2 us: gather_taps(): padded[1 + direction * shift_x:1 + direction * shift_x + width_x, 1 + dir...]
    pallas_call x0 -> x3, Pallas kernels: none -> 27.6 us  [the longest x1 24.1 us: work(): pl.pallas_call(work_kernel, grid_spec=pltpu.PrefetchScalarGridSpec(num_sc...]
    dot_general x10 -> x0, matrix products: 25 us -> none  [the longest x5 13.3 us: apply_taps(): result = jnp.dot(flattened, matrix, preferred_element_type=jnp.float32)]
    broadcast_in_dim x11 -> x2, local copies, waits for them, and re-layouts: 18.7 us -> 0.12 us  [spread_out(): copies = jnp.broadcast_to(rows[None], (lax.axis_size(axes),) + rows.shape)]
  transfers between devices with their start and end apart: 5 -> 2, of which waited for: 3 -> 1; matrix products, arithmetic and copies ran while one was open for 2% -> 0% of each run, Pallas kernels for 0% -> 2%
where the time goes in v2:
time: 86 us; the launch traced here: 85.8 us
  blocking collectives  45.7 us (53%)
  Pallas kernels  27.6 us (32%)
  starting transfers between devices  7.66 us (9%)
  waiting for transfers between devices  2.5 us (3%)
  other arithmetic  1.43 us (2%)
    all_to_all x2, blocking collectives, spread_out(): return lax.all_to_all(copies, axes, 0, 0, tiled=True)  28.1 us
    pallas_call x1, Pallas kernels, work(): pl.pallas_call(work_kernel, grid_spec=pltpu.PrefetchScalarGridSpec(num_sc...  24.1 us
    all_to_all x1, blocking collectives, scatter_sum(): split = lax.all_to_all(split, axes, 0, 0, tiled=True)  17.6 us
    ppermute x1, starting transfers between devices, per_device(): other = lax.ppermute(mine, 'core', swap)  4.33 us
    ppermute x1, starting transfers between devices, per_device(): other = lax.ppermute(other, 'core', swap)  3.33 us
    ppermute x1, waiting for transfers between devices, per_device(): other = lax.ppermute(other, 'core', swap)  2.5 us
    pallas_call x1, Pallas kernels, finish(): pl.pallas_call(finish_kernel, grid=(slots // 4,), in_specs=[blocks, pl.Bl...  2.05 us
  transfers between devices with their start and end apart: 2, of which 1 were waited for; matrix products, arithmetic and copies ran while one was open for 0% of the time, Pallas kernels for 2%

profile of v2, /device:TPU:1, one launch (start us, length us, event | category | flops | bytes accessed | tf_op | source)
XLA Modules:
  0.0 85.8 jit_solution(16194724528706650124)
XLA Ops:
  0.6 24.1 %work.1 = (bf16[16,8,16,512]{3,2,1,0:T(8,128)(2,1)}, bf16[4,128,512]{2,1,0:T(8,128)(2,1)}, f32[16,128,128]{2,1,0:T(8,128)}, f32[16,128,128]{2,1,0:T(8,128)}) custom-call(s32[128]{0:T(128)} %counts_ref.1, bf16[16,16,16,512]{3,2,1,0:T(8,128)(2,1)} %grad_ref.1, bf16[16,16,16,512]{3,2,1,0:T(8,128)(2,1)} %out_ref.1, bf16[16,8,8,512]{3,2,1,0:T(8,128)(2,1)} %deep_ref.1, ...), custom_call_target="tpu_custom_call" | custom-call | tf_op jit(solution)/shard_map/work/pallas_call | solution.py:372
  24.7 3.3 %collective-permute-start = (f32[16,128,128]{2,1,0:T(8,128)}, f32[16,128,128]{2,1,0:T(8,128)S(1)}, u32[]{:S(2)}, u32[]{:S(2)}) collective-permute-start(f32[16,128,128]{2,1,0:T(8,128)} %get-tuple-element.17), channel_id=1, source_target_pairs={{0,2},{2,0},{1,3},{3,1},{4,6},{6,4},{5,7},{7,5},{8,10},{10,8},{9,1... | collective-permute-start | bytes 3145736 | tf_op jit(solution)/shard_map/ppermute | solution.py:457
  28.1 2.5 %collective-permute-done = f32[16,128,128]{2,1,0:T(8,128)S(1)} collective-permute-done((f32[16,128,128]{2,1,0:T(8,128)}, f32[16,128,128]{2,1,0:T(8,128)S(1)}, u32[]{:S(2)}, u32[]{:S(2)}) %collective-permute-start) | collective-permute-done | bytes 1048608 | tf_op jit(solution)/shard_map/ppermute | solution.py:457
  30.6 1.3 %add_convert_fusion = bf16[16,128,128]{2,1,0:T(8,128)(2,1)S(1)} fusion(f32[16,128,128]{2,1,0:T(8,128)} %get-tuple-element.16, f32[16,128,128]{2,1,0:T(8,128)S(1)} %collective-permute-done), kind=kLoop, calls=%fused_computation.1 | loop fusion | flops 524288 | bytes 2621440 | tf_op jit(solution)/shard_map/convert_element_type | solution.py:458
  31.9 0.0 copy-start
  31.9 0.0 copy-start.1
  31.9 17.6 %all_to_all.15 = bf16[32,64,128]{2,1,0:T(8,128)(2,1)S(1)} all-to-all(bf16[32,64,128]{2,1,0:T(8,128)(2,1)S(1)} %bitcast.6), channel_id=1, replica_groups=mesh['zh'=4,'zl'=2,'xl'=2,'y'=4,'core'=2,'xh'=2] {'zl','xl','y','xh'}, dimensions={0} | all-to-all | bytes 1048576 | tf_op jit(solution)/shard_map/all_to_all | solution.py:438
  49.6 0.1 convert_reduce_fusion
  49.7 14.3 %all_to_all.16 = f32[4,64,128]{2,1,0:T(8,128)S(1)} all-to-all(f32[4,64,128]{2,1,0:T(8,128)S(1)} %broadcast_in_dim.4), channel_id=1, replica_groups=mesh['zh'=4,'zl'=2,'xl'=2,'y'=4,'core'=2,'xh'=2] {'zh'}, dimensions={0} | all-to-all | bytes 262144 | tf_op jit(solution)/shard_map/all_to_all | solution.py:444
  64.0 0.1 broadcast_in_dim.5
  64.1 13.7 %all_to_all.17 = bf16[32,64,128]{2,1,0:T(8,128)(2,1)S(1)} all-to-all(bf16[32,64,128]{2,1,0:T(8,128)(2,1)S(1)} %broadcast_in_dim.5), channel_id=1, replica_groups=mesh['zh'=4,'zl'=2,'xl'=2,'y'=4,'core'=2,'xh'=2] {'zl','xl','y','xh'}, dimensions={0} | all-to-all | bytes 1048576 | tf_op jit(solution)/shard_map/all_to_all | solution.py:444
  77.9 4.3 %collective-permute-start.1 = (bf16[2048,128]{1,0:T(8,128)(2,1)S(1)}, bf16[2048,128]{1,0:T(8,128)(2,1)S(1)}, u32[]{:S(2)}, u32[]{:S(2)}) collective-permute-start(bf16[2048,128]{1,0:T(8,128)(2,1)S(1)} %bitcast.4), channel_id=1, source_target_pairs={{0,2},{2,0},{1,3},{3,1},{4,6},{6,4},{5,7},{7,5},{8,10},{10,8},{9,1... | collective-permute-start | bytes 1572872 | tf_op jit(solution)/shard_map/ppermute | solution.py:463
  82.2 0.0 copy-done
  82.2 0.0 copy-done.1
  82.2 2.1 %finish.1 = bf16[16,8,16,512]{3,2,1,0:T(8,128)(2,1)} custom-call(bf16[16,8,16,512]{3,2,1,0:T(8,128)(2,1)S(1)} %copy-done, bf16[4,128,512]{2,1,0:T(8,128)(2,1)S(1)} %copy-done.1), custom_call_target="tpu_custom_call" | custom-call | flops 1048576 | bytes 8388608 | tf_op jit(solution)/shard_map/finish/pallas_call | solution.py:423
  84.3 0.0 collective-permute-done.1.refs_1_
  84.3 1.5 %unpack.1 = (f32[9,64,64]{2,1,0:T(8,128)}, f32[27,128,128]{2,1,0:T(8,128)}, f32[64,128]{1,0:T(8,128)}, f32[64,128]{1,0:T(8,128)}) custom-call(bf16[2048,128]{1,0:T(8,128)(2,1)S(1)} %bitcast.5, bf16[2048,128]{1,0:T(8,128)(2,1)S(1)} %collective-permute-done.1.refs_1_), custom_call_target="tpu_custom_call" | custom-call | tf_op jit(solution)/shard_map/unpack/pallas_call | solution.py:466
  (2 shorter events, 0.0 us)
Async XLA Ops:
  24.7 5.8 %collective-permute-start = (f32[16,128,128]{2,1,0:T(8,128)}, f32[16,128,128]{2,1,0:T(8,128)S(1)}, u32[]{:S(2)}, u32[]{:S(2)}) collective-permute-start(f32[16,128,128]{2,1,0:T(8,128)} %get-tuple-element.17), channel_id=1, source_target_pairs={{0,2},{2,0},{1,3},{3,1},{4,6},{6,4},{5,7},{7,5},{8,10},{10,8},{9,1... | collective-permute-start | bytes 3145736 | tf_op jit(solution)/shard_map/ppermute | solution.py:457
  31.9 50.3 %copy-start = (bf16[16,8,16,512]{3,2,1,0:T(8,128)(2,1)S(1)}, bf16[16,8,16,512]{3,2,1,0:T(8,128)(2,1)}, u32[]{:S(2)}) copy-start(bf16[16,8,16,512]{3,2,1,0:T(8,128)(2,1)} %get-tuple-element.15.skip_ref) | copy-start | bytes 6291460
  31.9 50.3 %copy-start.1 = (bf16[4,128,512]{2,1,0:T(8,128)(2,1)S(1)}, bf16[4,128,512]{2,1,0:T(8,128)(2,1)}, u32[]{:S(2)}) copy-start(bf16[4,128,512]{2,1,0:T(8,128)(2,1)} %get-tuple-element.19.pool_ref) | copy-start | bytes 1572868
  77.9 6.4 %collective-permute-start.1 = (bf16[2048,128]{1,0:T(8,128)(2,1)S(1)}, bf16[2048,128]{1,0:T(8,128)(2,1)S(1)}, u32[]{:S(2)}, u32[]{:S(2)}) collective-permute-start(bf16[2048,128]{1,0:T(8,128)(2,1)S(1)} %bitcast.4), channel_id=1, source_target_pairs={{0,2},{2,0},{1,3},{3,1},{4,6},{6,4},{5,7},{7,5},{8,10},{10,8},{9,1... | collective-permute-start | bytes 1572872 | tf_op jit(solution)/shard_map/ppermute | solution.py:463

commit v3 on v2

--- a/solution.py
+++ b/solution.py
@@ -19,6 +19,7 @@
 READER = ("zh", "zl", "xl", "y", "core")
 NEAR = ("zl", "xl", "y", "xh")
 FAR = "zh"
+AHEAD = 2
 UNITS = 16
 
 
@@ -45,20 +46,63 @@
 
 
 def work_kernel(
-    counts_ref, grad_ref, out_ref, deep_ref, pooled_ref, wdec_ref, wdeep_ref, wup_ref, wdown_ref,
-    skip_ref, pool_grad_ref, mine_ref, other_ref,
-    shifted, turned, toeplitz, spread, total, tile, parts,
-    start, rect, grads, pools, coarse, deep_turned, wfwd, wback, up_mat, down_mat, sems,
+    counts_ref, grad_hbm, out_hbm, deep_hbm, pooled_hbm, wdec_hbm, wdeep_hbm, wup_hbm, wdown_hbm,
+    skip_hbm, pool_grad_ref, mine_ref, other_ref,
+    grad_ref, out_ref, deep_ref, pooled_ref, wdec_ref, wdeep_ref, wup_ref, wdown_ref, skip_ref,
+    shifted, turned, toeplitz, spread, total, tile, parts, staged,
+    start, rect, grads, pools, coarse, deep_turned, wfwd, wback, up_mat, down_mat,
+    in_sems, weight_sems, wdeep_sems, skip_sems, part_sems,
 ):
-    step = pl.program_id(0)
-    last = pl.num_programs(0) - 1
     half = lax.axis_index("xh")
     core = lax.axis_index("core")
     count = counts_ref[lax.axis_index(READER)]
     sign = 1 - 2 * half
-
-    @pl.when(step == 0)
-    def _():
+    steps = grad_ref.shape[0] // 2
+
+    def loads(step):
+        two = pl.ds(2 * step, 2)
+        return [
+            pltpu.make_async_copy(
+                source.at[two, pl.ds(first, target.shape[1])], target.at[two], in_sems.at[k, step]
+            )
+            for k, (source, first, target) in enumerate(
+                [
+                    (grad_hbm, 5 * half, grad_ref),
+                    (out_hbm, 6 * half, out_ref),
+                    (deep_hbm, 3 * half, deep_ref),
+                    (pooled_hbm, 4 * half, pooled_ref),
+                ]
+            )
+        ]
+
+    def weight_load(step):
+        taps = pl.ds(3 * step, 3)
+        return pltpu.make_async_copy(wdeep_hbm.at[taps], wdeep_ref.at[taps], wdeep_sems.at[step])
+
+    def skip_store(step):
+        two = pl.ds(2 * step, 2)
+        return pltpu.make_async_copy(skip_ref.at[two], skip_hbm.at[two], skip_sems.at[step])
+
+    weights = [
+        pltpu.make_async_copy(source, target, weight_sems.at[k])
+        for k, (source, target) in enumerate(
+            [(wdec_hbm, wdec_ref), (wup_hbm, wup_ref), (wdown_hbm, wdown_ref)]
+        )
+    ]
+    def load_turn(turn):
+        for k in range(AHEAD):
+            for copy in loads(AHEAD * turn + k):
+                copy.start()
+            weight_load(AHEAD * turn + k).start()
+
+    for copy in weights:
+        copy.start()
+    load_turn(0)
+    weight_load(8).start()
+    for copy in weights:
+        copy.wait()
+
+    def prepare():
         tile[...] = jnp.zeros_like(tile)
         low_lane = lax.broadcasted_iota(jnp.int32, (64, 128), 1) < 64
         backs = []
@@ -82,10 +126,12 @@
         parts[1, UNITS - 1] = jnp.zeros((128, 128), F32)
         for dyi in range(3):
             for b in range(2):
-                shifted[dyi, b, 0] = jnp.zeros((BY, 512), BF16)
+                for buf in range(AHEAD):
+                    shifted[buf, dyi, b, 0] = jnp.zeros((BY, 512), BF16)
             rect[dyi, 0] = jnp.zeros((128, 512), BF16)
             grads[dyi, 0] = jnp.zeros((128, 512), BF16)
-        turned[0] = jnp.zeros((128, 128), BF16)
+        for buf in range(AHEAD):
+            turned[buf, 0] = jnp.zeros((128, 128), BF16)
         for z in range(4):
             deep_turned[0, z] = jnp.zeros((128, 128), BF16)
         up_mat[...] = jnp.zeros_like(up_mat)
@@ -96,10 +142,10 @@
             up_mat[lanes(z, 64), lanes(z)] = wup_ref[...]
             down_mat[lanes(z), lanes(z)] = down_t
 
-    def deep_weights():
+    def deep_weights(step):
         group = 3 * ((step // 3 - 1) * sign + 1) + step % 3
         zero = jnp.zeros((128, 128), BF16)
-        plain = [wdeep_ref[k] for k in range(3)]
+        plain = [wdeep_ref[3 * step + k] for k in range(3)]
         flipped = [value.T for value in plain]
         for zi in range(3):
             rows = pl.ds(pl.multiple_of((group * 3 + zi) * 128, 128), 128)
@@ -109,9 +155,8 @@
                     wfwd[g, rows, lanes(zo)] = plain[dz + 1] if abs(dz) <= 1 else zero
                     wback[g, rows, lanes(zo)] = flipped[1 - dz] if abs(dz) <= 1 else zero
 
-    @pl.when(step < last)
-    def _():
-        deep_weights()
+    def build(step, buf):
+        deep_weights(step)
         row_id = lax.broadcasted_iota(jnp.int32, (BY, 512), 0)
         not_first = row_id > 0
         not_last = row_id < BY - 1
@@ -119,26 +164,40 @@
         deep_last = row_id % 8 < 7
         rows = pl.ds(pl.multiple_of(step * 16, 16), 16)
         for b in range(2):
-            live = 2 * step + b < count
+            slot = 2 * step + b
+            live = slot < count
             for i in range(11):
-                value = grad_ref[b, half * 15 + sign * i].astype(F32)
+                value = grad_ref[slot, half * 10 + sign * i].astype(F32)
                 value = jnp.where(live, value, F32(0.0))
-                shifted[0, b, i + 1] = shift_rows(value, -1, not_last).astype(BF16)
-                shifted[1, b, i + 1] = value.astype(BF16)
-                shifted[2, b, i + 1] = shift_rows(value, 1, not_first).astype(BF16)
+                shifted[buf, 0, b, i + 1] = shift_rows(value, -1, not_last).astype(BF16)
+                shifted[buf, 1, b, i + 1] = value.astype(BF16)
+                shifted[buf, 2, b, i + 1] = shift_rows(value, 1, not_first).astype(BF16)
         for i in range(9):
             tiles = []
             for b in range(2):
-                row = out_ref[b, half * 15 + sign * i]
+                row = out_ref[2 * step + b, half * 9 + sign * i]
                 row = jnp.maximum(row, jnp.zeros_like(row))
                 tiles += [row[:, lanes(z)] for z in range(4)]
-            turned[i + 1] = cat(tiles, 0).T
-
+            turned[buf, i + 1] = cat(tiles, 0).T
+        for i in range(5):
+            source = half * 4 + sign * i
+            value = cat([deep_ref[2 * step + b, source].astype(F32) for b in range(2)], 0)
+            start[i, rows] = value.astype(BF16)
+            value = jnp.maximum(value, F32(0.0))
+            rect[0, i + 1, rows] = shift_rows(value, 1, deep_first).astype(BF16)
+            rect[1, i + 1, rows] = value.astype(BF16)
+            rect[2, i + 1, rows] = shift_rows(value, -1, deep_last).astype(BF16)
+            if i < 4:
+                source = half * 3 + sign * i
+                value = cat([pooled_ref[2 * step + b, source].astype(F32) for b in range(2)], 0)
+                pools[i, rows] = value.astype(BF16)
+
+    def back(buf):
         lhs = cat(
             [
                 cat(
                     [
-                        shifted[dyi, b, 2 * xp + w, :, lanes(z)]
+                        shifted[buf, dyi, b, 2 * xp + w, :, lanes(z)]
                         for b in range(2)
                         for xp in range(5)
                         for z in range(4)
@@ -150,32 +209,23 @@
             ],
             1,
         )
-        backed = dot(lhs, toeplitz[...])
-
-        lhs = cat([cat([turned[i + dxi] for i in range(8)], 1) for dxi in range(3)], 0)
+        return dot(lhs, toeplitz[...])
+
+    def outer(buf):
+        lhs = cat([cat([turned[buf, i + dxi] for i in range(8)], 1) for dxi in range(3)], 0)
         rhs = cat(
             [
-                cat([shifted[dyi, b, i + 1, :, lanes(z)] for dyi in range(3)], 1)
+                cat([shifted[buf, dyi, b, i + 1, :, lanes(z)] for dyi in range(3)], 1)
                 for i in range(8)
                 for b in range(2)
                 for z in range(4)
             ],
             0,
         )
-        total[...] += dot(lhs, rhs)
-
-        for i in range(5):
-            source = half * 7 + sign * i
-            value = cat([deep_ref[b, source].astype(F32) for b in range(2)], 0)
-            start[i, rows] = value.astype(BF16)
-            value = jnp.maximum(value, F32(0.0))
-            rect[0, i + 1, rows] = shift_rows(value, 1, deep_first).astype(BF16)
-            rect[1, i + 1, rows] = value.astype(BF16)
-            rect[2, i + 1, rows] = shift_rows(value, -1, deep_last).astype(BF16)
-            if i < 4:
-                value = cat([pooled_ref[b, source].astype(F32) for b in range(2)], 0)
-                pools[i, rows] = value.astype(BF16)
-
+        return dot(lhs, rhs)
+
+    def settle(step, buf, backed):
+        rows = pl.ds(pl.multiple_of(step * 16, 16), 16)
         low_lane = lax.broadcasted_iota(jnp.int32, (8, 128), 1) < 64
         for xp in range(5):
             pooled = []
@@ -187,20 +237,20 @@
                     conv = cat(
                         [backed[base + 16 * z : base + 16 * z + 16, lanes(xi)] for z in range(4)], 1
                     )
-                    gate = out_ref[b, half * 15 + sign * i].astype(F32) > 0
-                    value = shifted[1, b, i + 1].astype(F32) + jnp.where(gate, conv, F32(0.0))
+                    gate = out_ref[2 * step + b, half * 9 + sign * i].astype(F32) > 0
+                    value = shifted[buf, 1, b, i + 1].astype(F32) + jnp.where(gate, conv, F32(0.0))
                     value = value.astype(BF16)
                     if i < 8:
-                        skip_ref[b, half * 7 + sign * i] = value
+                        skip_ref[2 * step + b, half * 7 + sign * i] = value
                     both.append(value.astype(F32))
                 cell = both[0] + both[1]
                 quads = []
                 for z in range(4):
                     piece = cell[:, lanes(z)]
-                    slot = (xp * 2 + b) * 4 + z
-                    spread[slot] = piece + pltpu.roll(piece, 64, 1)
-                    even = spread[slot, pl.ds(0, 8, stride=2), :]
-                    quads.append(even + spread[slot, pl.ds(1, 8, stride=2), :])
+                    place = ((buf * 5 + xp) * 2 + b) * 4 + z
+                    spread[place] = piece + pltpu.roll(piece, 64, 1)
+                    even = spread[place, pl.ds(0, 8, stride=2), :]
+                    quads.append(even + spread[place, pl.ds(1, 8, stride=2), :])
                 pooled.append(
                     cat(
                         [jnp.where(low_lane, quads[2 * k], quads[2 * k + 1]) for k in range(2)], 1
@@ -208,9 +258,32 @@
                 )
             coarse[xp, rows] = cat(pooled, 0).astype(BF16)
 
-    @pl.when(step == last)
-    def _():
-        deep_weights()
+    def shallow(turn, carry):
+        mine = [AHEAD * turn + k for k in range(AHEAD)]
+
+        @pl.when(turn + 1 < steps // AHEAD)
+        def _():
+            load_turn(turn + 1)
+
+        for step in mine:
+            for copy in loads(step):
+                copy.wait()
+            weight_load(step).wait()
+        outers = []
+        for buf, step in enumerate(mine):
+            build(step, buf)
+        for buf, step in enumerate(mine):
+            backed = back(buf)
+            outers.append(outer(buf))
+            settle(step, buf, backed)
+        total[...] += sum(outers)
+        for step in mine:
+            skip_store(step).start()
+        return carry
+
+    def deep():
+        weight_load(8).wait()
+        deep_weights(8)
         row_id = lax.broadcasted_iota(jnp.int32, (128, 512), 0) % 8
         not_first = row_id > 0
         not_last = row_id < 7
@@ -280,6 +353,7 @@
                 parts[1, 12 + dyi, pl.ds(row, 32)] = summed
         for dyi in range(3):
             parts[1, 12 + dyi, 96:] = jnp.zeros((32, 128), F32)
+        stage_parts(0, UNITS - 1)
 
         outs = []
         for g in range(2):
@@ -299,15 +373,32 @@
         input_grad = cat(outs, 1)
         full = dot(cat([pools[i].T for i in range(4)], 1), input_grad)
         parts[0, UNITS - 1, 64:] = sum(full[lanes(z, 64), lanes(z)] for z in range(4))
-        send = pltpu.make_async_copy(parts.at[1 - core], other_ref, sems.at[0])
-        keep = pltpu.make_async_copy(parts.at[core], mine_ref, sems.at[1])
-        send.start()
-        keep.start()
+        stage_parts(UNITS - 1, 1)
         pool_grad = dot(input_grad, down_mat[...]).astype(BF16)
         for i in range(4):
             pool_grad_ref[i] = pool_grad[lanes(i)]
-        send.wait()
-        keep.wait()
+
+    def stage_parts(first, number):
+        for unit in range(first, first + number):
+            staged[unit] = parts[1 - core, unit].astype(BF16)
+        for copy in part_copies(first, number):
+            copy.start()
+
+    def part_copies(first, number):
+        units = pl.ds(first, number)
+        late = 0 if first == 0 else 2
+        return [
+            pltpu.make_async_copy(staged.at[units], other_ref.at[units], part_sems.at[late]),
+            pltpu.make_async_copy(parts.at[core, units], mine_ref.at[units], part_sems.at[late + 1]),
+        ]
+
+    prepare()
+    lax.fori_loop(0, steps // AHEAD, shallow, 0)
+    deep()
+    for k in range(steps):
+        skip_store(k).wait()
+    for copy in part_copies(0, UNITS - 1) + part_copies(UNITS - 1, 1):
+        copy.wait()
 
 
 def finish_kernel(skip_ref, pool_ref, done_ref, spread):
@@ -355,62 +446,53 @@
     down_ref[...] = block[64:]
 
 
-def whole(*shape):
-    return pl.BlockSpec(shape, lambda *step: (0,) * len(shape))
-
-
 def work(counts, dec_input, out_cotangent, pooled_skip, deep_input, dec_weight, deep_weight, up_weight, down_weight):
     slots = dec_input.shape[0]
     steps = slots // 2
-
-    def pair(*shape):
-        return pl.BlockSpec(
-            (2,) + shape, lambda s, counts: (jnp.minimum(s, steps - 1),) + (0,) * len(shape)
-        )
-
     anywhere = pl.BlockSpec(memory_space=pl.ANY)
     return pl.pallas_call(
         work_kernel,
-        grid_spec=pltpu.PrefetchScalarGridSpec(
-            num_scalar_prefetch=1,
-            grid=(steps + 1,),
-            in_specs=[
-                pair(BX, BY, 512),
-                pair(BX, BY, 512),
-                pair(8, 8, 512),
-                pair(8, 8, 256),
-                whole(9, 64, 64),
-                pl.BlockSpec((3, 128, 128), lambda s, counts: (s, 0, 0)),
-                whole(64, 128),
-                whole(64, 128),
-            ],
-            out_specs=[pair(8, BY, 512), whole(4, 8 * slots, 512), anywhere, anywhere],
-            scratch_shapes=[
-                pltpu.VMEM((3, 2, 12, BY, 512), BF16),
-                pltpu.VMEM((10, 128, 128), BF16),
-                pltpu.VMEM((1536, 256), BF16),
-                pltpu.VMEM((40, BY, 128), F32),
-                pltpu.VMEM((384, 384), F32),
-                pltpu.VMEM((128, 128), F32),
-                pltpu.VMEM((2, UNITS, 128, 128), F32),
-                pltpu.VMEM((5, 128, 512), BF16),
-                pltpu.VMEM((3, 6, 128, 512), BF16),
-                pltpu.VMEM((3, 6, 128, 512), BF16),
-                pltpu.VMEM((4, 128, 256), BF16),
-                pltpu.VMEM((5, 128, 256), BF16),
-                pltpu.VMEM((6, 4, 128, 128), BF16),
-                pltpu.VMEM((2, 3456, 256), BF16),
-                pltpu.VMEM((2, 3456, 256), BF16),
-                pltpu.VMEM((256, 512), BF16),
-                pltpu.VMEM((512, 512), BF16),
-                pltpu.SemaphoreType.DMA((2,)),
-            ],
-        ),
+        in_specs=[pl.BlockSpec(memory_space=pltpu.SMEM)] + [anywhere] * 8,
+        out_specs=[anywhere, pl.BlockSpec(memory_space=pltpu.VMEM), anywhere, anywhere],
+        scratch_shapes=[
+            pltpu.VMEM((slots, 11, BY, 512), BF16),
+            pltpu.VMEM((slots, 10, BY, 512), BF16),
+            pltpu.VMEM((slots, 5, 8, 512), BF16),
+            pltpu.VMEM((slots, 4, 8, 256), BF16),
+            pltpu.VMEM((9, 64, 64), BF16),
+            pltpu.VMEM((27, 128, 128), BF16),
+            pltpu.VMEM((64, 128), BF16),
+            pltpu.VMEM((64, 128), BF16),
+            pltpu.VMEM((slots, 8, BY, 512), BF16),
+            pltpu.VMEM((AHEAD, 3, 2, 12, BY, 512), BF16),
+            pltpu.VMEM((AHEAD, 10, 128, 128), BF16),
+            pltpu.VMEM((1536, 256), BF16),
+            pltpu.VMEM((40 * AHEAD, BY, 128), F32),
+            pltpu.VMEM((384, 384), F32),
+            pltpu.VMEM((128, 128), F32),
+            pltpu.VMEM((2, UNITS, 128, 128), F32),
+            pltpu.VMEM((UNITS, 128, 128), BF16),
+            pltpu.VMEM((5, 128, 512), BF16),
+            pltpu.VMEM((3, 6, 128, 512), BF16),
+            pltpu.VMEM((3, 6, 128, 512), BF16),
+            pltpu.VMEM((4, 128, 256), BF16),
+            pltpu.VMEM((5, 128, 256), BF16),
+            pltpu.VMEM((6, 4, 128, 128), BF16),
+            pltpu.VMEM((2, 3456, 256), BF16),
+            pltpu.VMEM((2, 3456, 256), BF16),
+            pltpu.VMEM((256, 512), BF16),
+            pltpu.VMEM((512, 512), BF16),
+            pltpu.SemaphoreType.DMA((4, steps)),
+            pltpu.SemaphoreType.DMA((3,)),
+            pltpu.SemaphoreType.DMA((9,)),
+            pltpu.SemaphoreType.DMA((steps,)),
+            pltpu.SemaphoreType.DMA((4,)),
+        ],
         out_shape=[
             jax.ShapeDtypeStruct((slots, 8, BY, 512), BF16),
             jax.ShapeDtypeStruct((4, 8 * slots, 512), BF16),
             jax.ShapeDtypeStruct((UNITS, 128, 128), F32),
-            jax.ShapeDtypeStruct((UNITS, 128, 128), F32),
+            jax.ShapeDtypeStruct((UNITS, 128, 128), BF16),
         ],
         compiler_params=pltpu.CompilerParams(vmem_limit_bytes=60 * 1024 * 1024),
         name="work",
@@ -455,7 +537,7 @@
         dec_weight, deep_weight, up_weight, down_weight,
     )
     other = lax.ppermute(other, "core", swap)
-    rows = (mine + other).astype(BF16).reshape(-1, 128)
+    rows = (mine + other.astype(F32)).astype(BF16).reshape(-1, 128)
     rows = scatter_sum(rows, NEAR)
     rows = spread_out(rows, FAR).sum(axis=0).astype(BF16)
     mine = spread_out(rows, NEAR).reshape(-1, 128)

time: 86 us -> 83.3 us (0.969)
  Pallas kernels: 27.6 us -> 25.7 us
    pallas_call x1, Pallas kernels: 24.1 us -> 22.1 us  [work(): pl.pallas_call(work_kernel, in_specs=[pl.BlockSpec(memory_space=pltpu.SME...]
where the time goes in v3:
time: 83.3 us; the launch traced here: 83 us
  blocking collectives  45.7 us (55%)
  Pallas kernels  25.7 us (31%)
  starting transfers between devices  7.66 us (9%)
  waiting for transfers between devices  1.75 us (2%)
  other arithmetic  1.45 us (2%)
    all_to_all x2, blocking collectives, spread_out(): return lax.all_to_all(copies, axes, 0, 0, tiled=True)  28.1 us
    pallas_call x1, Pallas kernels, work(): pl.pallas_call(work_kernel, in_specs=[pl.BlockSpec(memory_space=pltpu.SME...  22.1 us
    all_to_all x1, blocking collectives, scatter_sum(): split = lax.all_to_all(split, axes, 0, 0, tiled=True)  17.6 us
    ppermute x1, starting transfers between devices, per_device(): other = lax.ppermute(mine, 'core', swap)  4.33 us
    ppermute x1, starting transfers between devices, per_device(): other = lax.ppermute(other, 'core', swap)  3.32 us
    pallas_call x1, Pallas kernels, finish(): pl.pallas_call(finish_kernel, grid=(slots // 4,), in_specs=[blocks, pl.Bl...  2.05 us
    ppermute x1, waiting for transfers between devices, per_device(): other = lax.ppermute(other, 'core', swap)  1.75 us
  transfers between devices with their start and end apart: 2, of which 1 were waited for; matrix products, arithmetic and copies ran while one was open for 0% of the time, Pallas kernels for 2%

profile of v3, /device:TPU:1, one launch (start us, length us, event | category | flops | bytes accessed | tf_op | source)
XLA Modules:
  0.0 83.0 jit_solution(5453003772114227295)
XLA Ops:
  0.6 22.1 %work.1 = (bf16[16,8,16,512]{3,2,1,0:T(8,128)(2,1)}, bf16[4,128,512]{2,1,0:T(8,128)(2,1)}, f32[16,128,128]{2,1,0:T(8,128)}, bf16[16,128,128]{2,1,0:T(8,128)(2,1)}) custom-call(s32[128]{0:T(128)} %counts_ref.1, bf16[16,16,16,512]{3,2,1,0:T(8,128)(2,1)} %grad_hbm.1, bf16[16,16,16,512]{3,2,1,0:T(8,128)(2,1)} %out_hbm.1, bf16[16,8,8,512]{3,2,1,0:T(8,128)(2,1)} %deep_hbm.1, ...), custom_call_target="tpu_custom_call" | custom-call | tf_op jit(solution)/shard_map/work/pallas_call | solution.py:453
  22.8 3.3 %collective-permute-start = (bf16[16,128,128]{2,1,0:T(8,128)(2,1)}, bf16[16,128,128]{2,1,0:T(8,128)(2,1)S(1)}, u32[]{:S(2)}, u32[]{:S(2)}) collective-permute-start(bf16[16,128,128]{2,1,0:T(8,128)(2,1)} %get-tuple-element.17), channel_id=1, source_target_pairs={{0,2},{2,0},{1,3},{3,1},{4,6},{6,4},{5,7},{7,5},{8,10},{10,8},{9,1... | collective-permute-start | bytes 1572872 | tf_op jit(solution)/shard_map/ppermute | solution.py:539
  26.1 1.7 %collective-permute-done = bf16[16,128,128]{2,1,0:T(8,128)(2,1)S(1)} collective-permute-done((bf16[16,128,128]{2,1,0:T(8,128)(2,1)}, bf16[16,128,128]{2,1,0:T(8,128)(2,1)S(1)}, u32[]{:S(2)}, u32[]{:S(2)}) %collective-permute-start) | collective-permute-done | bytes 524320 | tf_op jit(solution)/shard_map/ppermute | solution.py:539
  27.8 1.4 %add_convert_fusion = bf16[16,128,128]{2,1,0:T(8,128)(2,1)S(1)} fusion(f32[16,128,128]{2,1,0:T(8,128)} %get-tuple-element.16, bf16[16,128,128]{2,1,0:T(8,128)(2,1)S(1)} %collective-permute-done), kind=kLoop, calls=%fused_computation.1 | loop fusion | flops 786432 | bytes 2097152 | tf_op jit(solution)/shard_map/convert_element_type | solution.py:540
  29.2 0.0 copy-start
  29.2 0.0 copy-start.1
  29.2 17.6 %all_to_all.15 = bf16[32,64,128]{2,1,0:T(8,128)(2,1)S(1)} all-to-all(bf16[32,64,128]{2,1,0:T(8,128)(2,1)S(1)} %bitcast.6), channel_id=1, replica_groups=mesh['zh'=4,'zl'=2,'xl'=2,'y'=4,'core'=2,'xh'=2] {'zl','xl','y','xh'}, dimensions={0} | all-to-all | bytes 1048576 | tf_op jit(solution)/shard_map/all_to_all | solution.py:520
  46.9 0.1 convert_reduce_fusion
  47.0 14.3 %all_to_all.16 = f32[4,64,128]{2,1,0:T(8,128)S(1)} all-to-all(f32[4,64,128]{2,1,0:T(8,128)S(1)} %broadcast_in_dim.4), channel_id=1, replica_groups=mesh['zh'=4,'zl'=2,'xl'=2,'y'=4,'core'=2,'xh'=2] {'zh'}, dimensions={0} | all-to-all | bytes 262144 | tf_op jit(solution)/shard_map/all_to_all | solution.py:526
  61.3 0.1 broadcast_in_dim.5
  61.4 13.7 %all_to_all.17 = bf16[32,64,128]{2,1,0:T(8,128)(2,1)S(1)} all-to-all(bf16[32,64,128]{2,1,0:T(8,128)(2,1)S(1)} %broadcast_in_dim.5), channel_id=1, replica_groups=mesh['zh'=4,'zl'=2,'xl'=2,'y'=4,'core'=2,'xh'=2] {'zl','xl','y','xh'}, dimensions={0} | all-to-all | bytes 1048576 | tf_op jit(solution)/shard_map/all_to_all | solution.py:526
  75.1 4.3 %collective-permute-start.1 = (bf16[2048,128]{1,0:T(8,128)(2,1)S(1)}, bf16[2048,128]{1,0:T(8,128)(2,1)S(1)}, u32[]{:S(2)}, u32[]{:S(2)}) collective-permute-start(bf16[2048,128]{1,0:T(8,128)(2,1)S(1)} %bitcast.4), channel_id=1, source_target_pairs={{0,2},{2,0},{1,3},{3,1},{4,6},{6,4},{5,7},{7,5},{8,10},{10,8},{9,1... | collective-permute-start | bytes 1572872 | tf_op jit(solution)/shard_map/ppermute | solution.py:545
  79.5 0.0 copy-done
  79.5 0.0 copy-done.1
  79.5 2.1 %finish.1 = bf16[16,8,16,512]{3,2,1,0:T(8,128)(2,1)} custom-call(bf16[16,8,16,512]{3,2,1,0:T(8,128)(2,1)S(1)} %copy-done, bf16[4,128,512]{2,1,0:T(8,128)(2,1)S(1)} %copy-done.1), custom_call_target="tpu_custom_call" | custom-call | flops 1048576 | bytes 8388608 | tf_op jit(solution)/shard_map/finish/pallas_call | solution.py:505
  81.5 0.0 collective-permute-done.1.refs_1_
  81.5 1.5 %unpack.1 = (f32[9,64,64]{2,1,0:T(8,128)}, f32[27,128,128]{2,1,0:T(8,128)}, f32[64,128]{1,0:T(8,128)}, f32[64,128]{1,0:T(8,128)}) custom-call(bf16[2048,128]{1,0:T(8,128)(2,1)S(1)} %bitcast.5, bf16[2048,128]{1,0:T(8,128)(2,1)S(1)} %collective-permute-done.1.refs_1_), custom_call_target="tpu_custom_call" | custom-call | tf_op jit(solution)/shard_map/unpack/pallas_call | solution.py:548
  (2 shorter events, 0.0 us)
Async XLA Ops:
  22.8 5.1 %collective-permute-start = (bf16[16,128,128]{2,1,0:T(8,128)(2,1)}, bf16[16,128,128]{2,1,0:T(8,128)(2,1)S(1)}, u32[]{:S(2)}, u32[]{:S(2)}) collective-permute-start(bf16[16,128,128]{2,1,0:T(8,128)(2,1)} %get-tuple-element.17), channel_id=1, source_target_pairs={{0,2},{2,0},{1,3},{3,1},{4,6},{6,4},{5,7},{7,5},{8,10},{10,8},{9,1... | collective-permute-start | bytes 1572872 | tf_op jit(solution)/shard_map/ppermute | solution.py:539
  29.2 50.3 %copy-start = (bf16[16,8,16,512]{3,2,1,0:T(8,128)(2,1)S(1)}, bf16[16,8,16,512]{3,2,1,0:T(8,128)(2,1)}, u32[]{:S(2)}) copy-start(bf16[16,8,16,512]{3,2,1,0:T(8,128)(2,1)} %get-tuple-element.15.skip_ref) | copy-start | bytes 6291460
  29.2 50.3 %copy-start.1 = (bf16[4,128,512]{2,1,0:T(8,128)(2,1)S(1)}, bf16[4,128,512]{2,1,0:T(8,128)(2,1)}, u32[]{:S(2)}) copy-start(bf16[4,128,512]{2,1,0:T(8,128)(2,1)} %get-tuple-element.19.pool_ref) | copy-start | bytes 1572868
  75.1 6.4 %collective-permute-start.1 = (bf16[2048,128]{1,0:T(8,128)(2,1)S(1)}, bf16[2048,128]{1,0:T(8,128)(2,1)S(1)}, u32[]{:S(2)}, u32[]{:S(2)}) collective-permute-start(bf16[2048,128]{1,0:T(8,128)(2,1)S(1)} %bitcast.4), channel_id=1, source_target_pairs={{0,2},{2,0},{1,3},{3,1},{4,6},{6,4},{5,7},{7,5},{8,10},{10,8},{9,1... | collective-permute-start | bytes 1572872 | tf_op jit(solution)/shard_map/ppermute | solution.py:545
